TPU v7x, 512 devices: a whole 4x4x16 slice. The times are simulated.
512 devices in a mesh: ctx: 16 (over x, y_hi, core), head: 32 (over z, y_lo).
Axes of the slice: x: 4, y: 4 (y_hi: 2, y_lo: 2; y = y_hi * 2 + y_lo), z: 16, core: 2. Of those that a mesh axis runs over, the one named last changes fastest.
Arguments:
- query: bfloat16 [65536, 4096], P(('ctx', 'head')), may hold values from -13 to 13
- key: bfloat16 [65536, 512], P(('ctx', 'head')), may hold values from -8 to 8
- value: bfloat16 [65536, 512], P(('ctx', 'head')), may hold values from -6 to 6
- attn_out: bfloat16 [65536, 4096], P(('ctx', 'head')), may hold values from -6 to 6
- out_grad: bfloat16 [65536, 4096], P(('ctx', 'head')), may hold values from -6 to 6
- segments: int32 [65536], P(('ctx', 'head')), may hold values from 0 to 255, never falling along the last dimension, each value on 1 to 512 neighbouring positions
Outputs:
- query_grad: bfloat16 [65536, 4096], P(('ctx', 'head'))
- key_grad: bfloat16 [65536, 512], P(('ctx', 'head'))
- value_grad: bfloat16 [65536, 512], P(('ctx', 'head'))
Inputs may be any that keep to these rules, and one draw needn't show every extreme that they name: `segments`: never falls along positions; each document spans at most 512 positions, and one spans exactly 512.
All inputs are finite; a program needn't handle non-finite values.
Results may differ from a plain program's by a relative error of at most 0.0057.
Values may be sent and summed in bfloat16 or wider, within the bound.
No kernel may reach another device: no remote copies, remote signals or barrier semaphores. Data moves between devices by JAX's collectives and lax.ppermute only.
A program may use at most 64 MiB of HBM per device.

v0:
```python
import jax
import jax.numpy as jnp
from jax import lax
from jax.sharding import PartitionSpec as P

HEAD_DIM = 128
MOST = 512


def from_behind(value, axis, steps):
    count = lax.axis_size(axis)
    leading, last = (max(0, -steps), min(count, count - steps))
    return lax.ppermute(value, axis, [(source, source + steps) for source in range(leading, last)])


def block_math(q_blk, k_blk, v_blk, g_blk, delta_blk, allowed, scale):
    s = jnp.einsum("qhd,khd->hqk", q_blk, k_blk, preferred_element_type=jnp.float32) * scale
    s = jnp.where(allowed[None], s, -jnp.inf)
    top = jnp.max(s, axis=-1, keepdims=True)
    total = jnp.sum(jnp.exp(s - top), axis=-1, keepdims=True)
    prob = jnp.exp(s - (top + jnp.log(total)))
    dprob = jnp.einsum("qhd,khd->hqk", g_blk, v_blk, preferred_element_type=jnp.float32)
    dscore = prob * (dprob - jnp.transpose(delta_blk)[:, :, None])
    prob_low = prob.astype(jnp.bfloat16)
    dscore_low = dscore.astype(jnp.bfloat16)
    dq = jnp.einsum("hqk,khd->qhd", dscore_low, k_blk, preferred_element_type=jnp.float32) * scale
    dk = jnp.einsum("hqk,qhd->khd", dscore_low, q_blk, preferred_element_type=jnp.float32) * scale
    dv = jnp.einsum("hqk,qhd->khd", prob_low, g_blk, preferred_element_type=jnp.float32)
    return (dq.astype(jnp.bfloat16), dk, dv)


def per_device(query, key, value, attn_out, out_grad, segments):
    tok = query.shape[0]
    heads = query.shape[1] // HEAD_DIM
    kv_heads = key.shape[1] // HEAD_DIM
    group = heads // kv_heads
    span = MOST
    scale = HEAD_DIM ** (-0.5)
    q3 = query.reshape(tok, heads, HEAD_DIM)
    g3 = out_grad.reshape(tok, heads, HEAD_DIM)
    o3 = attn_out.reshape(tok, heads, HEAD_DIM)
    k3 = jnp.repeat(key.reshape(tok, kv_heads, HEAD_DIM), group, axis=1)
    v3 = jnp.repeat(value.reshape(tok, kv_heads, HEAD_DIM), group, axis=1)
    q_loc, k_loc, v_loc, g_loc, o_loc = (
        lax.all_to_all(q3, "head", split_axis=1, concat_axis=0, tiled=True),
        lax.all_to_all(k3, "head", split_axis=1, concat_axis=0, tiled=True),
        lax.all_to_all(v3, "head", split_axis=1, concat_axis=0, tiled=True),
        lax.all_to_all(g3, "head", split_axis=1, concat_axis=0, tiled=True),
        lax.all_to_all(o3, "head", split_axis=1, concat_axis=0, tiled=True),
    )
    delta = jnp.sum(g_loc.astype(jnp.float32) * o_loc.astype(jnp.float32), axis=2)
    block_rows = q_loc.shape[0]
    local_heads = q_loc.shape[1]
    nblocks = block_rows // span
    seg_own = lax.all_gather(segments, "head", axis=0, tiled=True)
    seg_rim = from_behind(seg_own[block_rows - span :], "ctx", 1)
    base = lax.axis_index("ctx") * block_rows
    rim_k, rim_v = from_behind((k_loc[block_rows - span :], v_loc[block_rows - span :]), "ctx", 1)
    k_ext = jnp.concatenate([rim_k, k_loc], axis=0)
    v_ext = jnp.concatenate([rim_v, v_loc], axis=0)
    seg_ext = jnp.concatenate([seg_rim, seg_own], axis=0)
    offsets = jnp.arange(span, dtype=jnp.int32)
    wide_offsets = jnp.arange(2 * span, dtype=jnp.int32)

    def one_block(block):
        start = block * span
        q_blk = lax.dynamic_slice_in_dim(q_loc, start, span, 0)
        g_blk = lax.dynamic_slice_in_dim(g_loc, start, span, 0)
        d_blk = lax.dynamic_slice_in_dim(delta, start, span, 0)
        k_blk = lax.dynamic_slice_in_dim(k_ext, start, 2 * span, 0)
        v_blk = lax.dynamic_slice_in_dim(v_ext, start, 2 * span, 0)
        seg_q = lax.dynamic_slice_in_dim(seg_own, start, span, 0)
        seg_k = lax.dynamic_slice_in_dim(seg_ext, start, 2 * span, 0)
        q_pos = base + start + offsets
        k_pos = base + start - span + wide_offsets
        allowed = (
            (seg_q[:, None] == seg_k[None, :])
            & (k_pos[None, :] <= q_pos[:, None])
            & (k_pos[None, :] >= 0)
        )
        return block_math(q_blk, k_blk, v_blk, g_blk, d_blk, allowed, scale)

    dq_blocks, dk_terms, dv_terms = lax.map(one_block, jnp.arange(nblocks, dtype=jnp.int32))
    empty = jnp.zeros((1, span, local_heads, HEAD_DIM), jnp.float32)
    dk_ext = jnp.concatenate([dk_terms[:, :span], empty], axis=0) + jnp.concatenate(
        [empty, dk_terms[:, span:]], axis=0
    )
    dv_ext = jnp.concatenate([dv_terms[:, :span], empty], axis=0) + jnp.concatenate(
        [empty, dv_terms[:, span:]], axis=0
    )
    back_k, back_v = from_behind((dk_ext[0], dv_ext[0]), "ctx", -1)
    own_k = dk_ext[1:].at[nblocks - 1].add(back_k).reshape(block_rows, local_heads, HEAD_DIM)
    own_v = dv_ext[1:].at[nblocks - 1].add(back_v).reshape(block_rows, local_heads, HEAD_DIM)
    dq_loc = dq_blocks.reshape(block_rows, local_heads, HEAD_DIM)
    dq_tok, dk_tok, dv_tok = (
        lax.all_to_all(dq_loc, "head", split_axis=0, concat_axis=1, tiled=True),
        lax.all_to_all(own_k.astype(jnp.bfloat16), "head", split_axis=0, concat_axis=1, tiled=True),
        lax.all_to_all(own_v.astype(jnp.bfloat16), "head", split_axis=0, concat_axis=1, tiled=True),
    )
    key_grad = dk_tok.astype(jnp.float32).reshape(tok, kv_heads, group, HEAD_DIM).sum(axis=2)
    value_grad = dv_tok.astype(jnp.float32).reshape(tok, kv_heads, group, HEAD_DIM).sum(axis=2)
    return (
        dq_tok.reshape(tok, heads * HEAD_DIM),
        key_grad.astype(jnp.bfloat16).reshape(tok, kv_heads * HEAD_DIM),
        value_grad.astype(jnp.bfloat16).reshape(tok, kv_heads * HEAD_DIM),
    )


def solution(mesh):
    placed = (
        P(("ctx", "head"), None),
        P(("ctx", "head"), None),
        P(("ctx", "head"), None),
        P(("ctx", "head"), None),
        P(("ctx", "head"), None),
        P(("ctx", "head")),
    )
    return jax.shard_map(
        per_device,
        mesh=mesh,
        in_specs=placed,
        out_specs=(P(("ctx", "head"), None), P(("ctx", "head"), None), P(("ctx", "head"), None)),
        check_vma=False,
    )
```

profile of v0, /device:TPU:6, one launch (start us, length us, event | category | flops | bytes accessed | tf_op | source)
XLA Modules:
  0.0 689.0 jit_solution(13808425033847957924)
XLA Ops:
  2.8 16.5 %all-to-all-start = ((bf16[128,32,128]{2,0,1:T(8,128)(2,1)}), bf16[128,32,128]{2,0,1:T(8,128)(2,1)S(1)}, u32[]{:S(2)}, u32[]{:S(2)}) async-start(bf16[128,32,128]{2,0,1:T(8,128)(2,1)} %bitcast), calls=%async_computation | async-start | bytes 2097152 | tf_op jit(solution)/shard_map/all_to_all | solution.py:46
  20.6 52.5 %all-to-all-done = bf16[128,32,128]{2,0,1:T(8,128)(2,1)S(1)} async-done(((bf16[128,32,128]{2,0,1:T(8,128)(2,1)}), bf16[128,32,128]{2,0,1:T(8,128)(2,1)S(1)}, u32[]{:S(2)}, u32[]{:S(2)}) %all-to-all-start) | async-done | bytes 1048608 | tf_op jit(solution)/shard_map/all_to_all | solution.py:46
  73.1 5.1 all-to-all-start.1
  79.5 52.5 %all-to-all-done.1 = bf16[128,32,128]{0,2,1:T(8,128)(2,1)S(1)} async-done(((bf16[128,32,128]{0,2,1:T(8,128)(2,1)}), bf16[128,32,128]{0,2,1:T(8,128)(2,1)S(1)}, u32[]{:S(2)}, u32[]{:S(2)}) %all-to-all-start.1) | async-done | bytes 1048608 | tf_op jit(solution)/shard_map/all_to_all | solution.py:45
  132.9 4.8 all-to-all-start.2
  137.7 53.8 %all-to-all-done.2 = bf16[128,32,128]{0,2,1:T(8,128)(2,1)S(1)} async-done(((bf16[128,32,128]{0,2,1:T(8,128)(2,1)}), bf16[128,32,128]{0,2,1:T(8,128)(2,1)S(1)}, u32[]{:S(2)}, u32[]{:S(2)}) %all-to-all-start.2) | async-done | bytes 1048608 | tf_op jit(solution)/shard_map/all_to_all | solution.py:48
  192.7 4.9 all-to-all-start.3
  197.6 2.3 copy.70
  199.9 51.5 %all-to-all-done.3 = bf16[128,32,128]{2,0,1:T(8,128)(2,1)S(1)} async-done(((bf16[128,32,128]{2,0,1:T(8,128)(2,1)}), bf16[128,32,128]{2,0,1:T(8,128)(2,1)S(1)}, u32[]{:S(2)}, u32[]{:S(2)}) %all-to-all-start.3) | async-done | bytes 1048608 | tf_op jit(solution)/shard_map/all_to_all | solution.py:47
  251.4 4.9 all-to-all-start.4
  256.3 98.9 %all-gather = s32[32,1,128]{2,1,0:T(1,128)S(1)} all-gather(s32[1,1,128]{2,1,0:T(1,128)S(1)} %bitcast.189), channel_id=1, replica_groups=mesh['ctx'=16,'head'=32] {'head'}, dimensions={0}, use_global_device_ids=true | all-gather | bytes 16896 | tf_op jit(solution)/shard_map/all_gather | solution.py:55
  355.3 1.9 collective-permute-start.1
  357.2 5.3 collective-permute-done.1
  363.2 1.9 collective-permute-start
  365.1 2.3 copy.66
  369.4 4.0 collective-permute-start.2
  373.4 2.2 fusion.34
  375.7 2.6 collective-permute-done.2
  378.3 2.3 pad_maximum_fusion.1
  380.6 120.9 %while.19 = (s32[]{:T(128)}, bf16[8,512,1,128]{3,1,0,2:T(8,128)(2,1)}, f32[8,1024,1,128]{3,1,2,0:T(8,128)}, f32[8,1024,1,128]{3,1,2,0:T(8,128)}, s32[8]{0:T(128)...) while((s32[]{:T(128)}, ...), condition=%wide.region_4.5_spmd.clone, body=%wide.region_1.4_spmd.clone.sunk | while | flops 679218176 | bytes 28236180 | solution.py:83
  382.9 1.7 fusion.71
  385.8 1.5 multiply_convert_fusion.2
  389.6 2.3 convolution_bitcast_fusion.2
  398.0 1.7 fusion.71
  400.9 1.5 multiply_convert_fusion.2
  404.7 2.3 convolution_bitcast_fusion.2
  413.1 1.7 fusion.71
  416.0 1.5 multiply_convert_fusion.2
  417.5 1.4 fusion.72
  419.8 2.3 convolution_bitcast_fusion.2
  428.2 1.7 fusion.71
  431.1 1.5 multiply_convert_fusion.2
  434.9 2.3 convolution_bitcast_fusion.2
  443.3 1.7 fusion.71
  446.2 1.5 multiply_convert_fusion.2
  450.0 2.3 convolution_bitcast_fusion.2
  458.5 1.7 fusion.71
  461.3 1.5 multiply_convert_fusion.2
  462.8 1.4 fusion.72
  465.1 2.3 convolution_bitcast_fusion.2
  473.5 1.7 fusion.71
  476.4 1.5 multiply_convert_fusion.2
  480.2 2.3 convolution_bitcast_fusion.2
  488.7 1.7 fusion.71
  491.5 1.5 multiply_convert_fusion.2
  495.3 2.3 convolution_bitcast_fusion.2
  502.0 2.7 reduce.18
  505.8 13.5 %all-to-all-start.5 = ((bf16[32,2,8192]{2,1,0:T(2,128)(2,1)}), bf16[32,2,8192]{2,1,0:T(2,128)(2,1)}, u32[]{:S(2)}, u32[]{:S(2)}) async-start(bf16[32,2,8192]{2,1,0:T(2,128)(2,1)} %reshape.295), calls=%async_computation.5 | async-start | bytes 2097152 | tf_op jit(solution)/shard_map/all_to_all | solution.py:96
  519.3 5.5 fusion.46
  524.8 1.9 collective-permute-start.3
  527.0 3.8 collective-permute-done.3
  530.8 2.1 reduce.19
  532.9 2.1 reshape.297
  535.0 37.2 %all-to-all-done.5 = bf16[32,2,8192]{2,1,0:T(2,128)(2,1)} async-done(((bf16[32,2,8192]{2,1,0:T(2,128)(2,1)}), bf16[32,2,8192]{2,1,0:T(2,128)(2,1)}, u32[]{:S(2)}, u32[]{:S(2)}) %all-to-all-start.5) | async-done | bytes 1048608 | tf_op jit(solution)/shard_map/all_to_all | solution.py:96
  572.2 4.7 all-to-all-start.6
  578.0 2.5 collective-permute-start.4
  580.8 3.8 collective-permute-done.4
  584.6 1.4 reduce.20
  587.2 42.5 %all-to-all-done.6 = bf16[32,2,8192]{2,1,0:T(2,128)(2,1)} async-done(((bf16[32,2,8192]{2,1,0:T(2,128)(2,1)}), bf16[32,2,8192]{2,1,0:T(2,128)(2,1)}, u32[]{:S(2)}, u32[]{:S(2)}) %all-to-all-start.6) | async-done | bytes 1048608 | tf_op jit(solution)/shard_map/all_to_all | solution.py:97
  629.7 3.9 all-to-all-start.7
  633.6 4.3 reshape.296
  639.0 1.6 copy.73
  641.9 4.3 reshape.298
  649.7 37.1 %all-to-all-done.7 = bf16[32,2,8192]{2,1,0:T(2,128)(2,1)S(1)} async-done(((bf16[32,2,8192]{2,1,0:T(2,128)(2,1)}), bf16[32,2,8192]{2,1,0:T(2,128)(2,1)S(1)}, u32[]{:S(2)}, u32[]{:S(2)}) %all-to-all-start.7) | async-done | bytes 1048608 | tf_op jit(solution)/shard_map/all_to_all | solution.py:98
  (214 shorter events, 89.5 us)
Async XLA Ops:
  0.6 0.9 copy-start
  0.6 18.6 %copy-start.7 = (bf16[128,4096]{1,0:T(8,128)(2,1)S(1)}, bf16[128,4096]{1,0:T(8,128)(2,1)}, u32[]{:S(2)}) copy-start(bf16[128,4096]{1,0:T(8,128)(2,1)} %param.12) | copy-start | bytes 3145732
  2.8 70.3 %all-to-all-start = ((bf16[128,32,128]{2,0,1:T(8,128)(2,1)}), bf16[128,32,128]{2,0,1:T(8,128)(2,1)S(1)}, u32[]{:S(2)}, u32[]{:S(2)}) async-start(bf16[128,32,128]{2,0,1:T(8,128)(2,1)} %bitcast), calls=%async_computation | async-start | bytes 2097152 | tf_op jit(solution)/shard_map/all_to_all | solution.py:46
  19.3 58.9 %copy-start.8 = (bf16[128,4096]{1,0:T(8,128)(2,1)S(1)}, bf16[128,4096]{1,0:T(8,128)(2,1)}, u32[]{:S(2)}) copy-start(bf16[128,4096]{1,0:T(8,128)(2,1)} %param.16) | copy-start | bytes 3145732
  73.1 58.9 %all-to-all-start.1 = ((bf16[128,32,128]{0,2,1:T(8,128)(2,1)}), bf16[128,32,128]{0,2,1:T(8,128)(2,1)S(1)}, u32[]{:S(2)}, u32[]{:S(2)}) async-start(bf16[128,32,128]{0,2,1:T(8,128)(2,1)} %bitcast.9), calls=%async_computation.1 | async-start | bytes 2097152 | tf_op jit(solution)/shard_map/all_to_all | solution.py:45
  78.2 59.5 %copy-start.9 = (bf16[128,512]{1,0:T(8,128)(2,1)S(1)}, bf16[128,512]{1,0:T(8,128)(2,1)}, u32[]{:S(2)}) copy-start(bf16[128,512]{1,0:T(8,128)(2,1)} %param.14) | copy-start | bytes 393220
  131.9 1.0 copy-start.6
  132.9 58.6 %all-to-all-start.2 = ((bf16[128,32,128]{0,2,1:T(8,128)(2,1)}), bf16[128,32,128]{0,2,1:T(8,128)(2,1)S(1)}, u32[]{:S(2)}, u32[]{:S(2)}) async-start(bf16[128,32,128]{0,2,1:T(8,128)(2,1)} %bitcast.13), calls=%async_computation.2 | async-start | bytes 2097152 | tf_op jit(solution)/shard_map/all_to_all | solution.py:48
  192.7 58.7 %all-to-all-start.3 = ((bf16[128,32,128]{2,0,1:T(8,128)(2,1)}), bf16[128,32,128]{2,0,1:T(8,128)(2,1)S(1)}, u32[]{:S(2)}, u32[]{:S(2)}) async-start(bf16[128,32,128]{2,0,1:T(8,128)(2,1)} %bitcast.177), calls=%async_computation.3 | async-start | bytes 2097152 | tf_op jit(solution)/shard_map/all_to_all | solution.py:47
  197.6 58.7 %copy-start.10 = (s32[128]{0:T(128)S(1)}, s32[128]{0:T(128)}, u32[]{:S(2)}) copy-start(s32[128]{0:T(128)} %param.17) | copy-start | bytes 1540
  251.4 117.4 %copy-start.5 = (bf16[128,32,128]{2,0,1:T(8,128)(2,1)}, bf16[128,32,128]{2,0,1:T(8,128)(2,1)S(1)}, u32[]{:S(2)}) copy-start(bf16[128,32,128]{2,0,1:T(8,128)(2,1)S(1)} %all-to-all-done.3) | copy-start | bytes 3145732
  251.4 122.1 %all-to-all-start.4 = ((bf16[128,32,128]{0,2,1:T(8,128)(2,1)}), bf16[128,32,128]{0,2,1:T(8,128)(2,1)}, u32[]{:S(2)}, u32[]{:S(2)}) async-start(bf16[128,32,128]{0,2,1:T(8,128)(2,1)} %bitcast.176), calls=%async_computation.4 | async-start | bytes 2097152 | tf_op jit(solution)/shard_map/all_to_all | solution.py:49
  355.3 7.3 %collective-permute-start.1 = (s32[512]{0:T(512)S(1)}, s32[512]{0:T(512)S(1)}, u32[]{:S(2)}, u32[]{:S(2)}) collective-permute-start(s32[512]{0:T(512)S(1)} %bitcast.188), channel_id=1, source_target_pairs={{0,32},{32,64},{64,96},{96,128},{128,160},{160,192},{192,224},{224... | collective-permute-start | bytes 6152 | tf_op jit(solution)/shard_map/ppermute | solution.py:13
  363.2 12.5 %collective-permute-start = (bf16[512,1,128]{2,0,1:T(8,128)(2,1)S(1)}, bf16[512,1,128]{2,0,1:T(8,128)(2,1)S(1)}, u32[]{:S(2)}, u32[]{:S(2)}) collective-permute-start(bf16[512,1,128]{2,0,1:T(8,128)(2,1)S(1)} %bitcast.184), channel_id=1, source_target_pairs={{0,32},{32,64},{64,96},{96,128},{128,160},{160,192},{192,224},{224... | collective-permute-start | bytes 393224 | tf_op jit(solution)/shard_map/ppermute | solution.py:13
  369.4 8.9 %collective-permute-start.2 = (bf16[512,1,128]{2,0,1:T(8,128)(2,1)}, bf16[512,1,128]{2,0,1:T(8,128)(2,1)S(1)}, u32[]{:S(2)}, u32[]{:S(2)}) collective-permute-start(bf16[512,1,128]{2,0,1:T(8,128)(2,1)} %bitcast.20), channel_id=1, source_target_pairs={{0,32},{32,64},{64,96},{96,128},{128,160},{160,192},{192,224},{224... | collective-permute-start | bytes 393224 | tf_op jit(solution)/shard_map/ppermute | solution.py:13
  380.6 4.0 copy-start.3
  394.4 1.4 copy-start.4
  395.8 4.0 copy-start.3
  409.5 1.4 copy-start.4
  410.9 4.0 copy-start.3
  424.6 1.4 copy-start.4
  426.0 4.0 copy-start.3
  439.7 1.4 copy-start.4
  441.1 4.0 copy-start.3
  454.8 1.4 copy-start.4
  456.2 4.0 copy-start.3
  469.9 1.4 copy-start.4
  471.3 4.0 copy-start.3
  485.0 1.4 copy-start.4
  486.4 4.0 copy-start.3
  500.1 1.4 copy-start.4
  505.8 66.4 %all-to-all-start.5 = ((bf16[32,2,8192]{2,1,0:T(2,128)(2,1)}), bf16[32,2,8192]{2,1,0:T(2,128)(2,1)}, u32[]{:S(2)}, u32[]{:S(2)}) async-start(bf16[32,2,8192]{2,1,0:T(2,128)(2,1)} %reshape.295), calls=%async_computation.5 | async-start | bytes 2097152 | tf_op jit(solution)/shard_map/all_to_all | solution.py:96
  524.8 6.0 collective-permute-start.3
  572.2 57.4 %all-to-all-start.6 = ((bf16[32,2,8192]{2,1,0:T(2,128)(2,1)}), bf16[32,2,8192]{2,1,0:T(2,128)(2,1)}, u32[]{:S(2)}, u32[]{:S(2)}) async-start(bf16[32,2,8192]{2,1,0:T(2,128)(2,1)} %reshape.297), calls=%async_computation.6 | async-start | bytes 2097152 | tf_op jit(solution)/shard_map/all_to_all | solution.py:97
  576.9 3.6 copy-start.2
  578.0 6.5 collective-permute-start.4
  629.7 57.1 %all-to-all-start.7 = ((bf16[32,2,8192]{2,1,0:T(2,128)(2,1)}), bf16[32,2,8192]{2,1,0:T(2,128)(2,1)S(1)}, u32[]{:S(2)}, u32[]{:S(2)}) async-start(bf16[32,2,8192]{2,1,0:T(2,128)(2,1)} %reshape.299), calls=%async_computation.7 | async-start | bytes 2097152 | tf_op jit(solution)/shard_map/all_to_all | solution.py:98
  686.8 2.3 copy-start.1
where the time goes:
time: 694 us; the launch traced here: 689 us
  waiting for transfers between devices  342 us (49%)
  blocking collectives  98.9 us (14%)
  local copies, waits for them, and re-layouts  85.5 us (12%)
  starting transfers between devices  70.4 us (10%)
  matrix products  66.1 us (10%)
  other arithmetic  18.6 us (3%)
    all_gather x1, blocking collectives, per_device(): seg_own = lax.all_gather(segments, 'head', axis=0, tiled=True)  98.9 us
    all_to_all x1, waiting for transfers between devices, per_device(): lax.all_to_all(g3, 'head', split_axis=1, concat_axis=0, tiled=True)  53.8 us
    all_to_all x1, waiting for transfers between devices, per_device(): lax.all_to_all(k3, 'head', split_axis=1, concat_axis=0, tiled=True)  52.5 us
    all_to_all x1, waiting for transfers between devices, per_device(): lax.all_to_all(q3, 'head', split_axis=1, concat_axis=0, tiled=True)  52.5 us
    all_to_all x1, waiting for transfers between devices, per_device(): lax.all_to_all(v3, 'head', split_axis=1, concat_axis=0, tiled=True)  51.5 us
    all_to_all x1, waiting for transfers between devices, per_device(): lax.all_to_all(own_k.astype(jnp.bfloat16), 'head', split_axis=0, concat_a...  42.5 us
    all_to_all x1, waiting for transfers between devices, per_device(): lax.all_to_all(dq_loc, 'head', split_axis=0, concat_axis=1, tiled=True)  37.2 us
    all_to_all x1, waiting for transfers between devices, per_device(): lax.all_to_all(own_v.astype(jnp.bfloat16), 'head', split_axis=0, concat_a...  37.1 us
  transfers between devices with their start and end apart: 13, of which 11 were waited for; matrix products, arithmetic and copies ran while one was open for 6% of the time, Pallas kernels for 0%

commit v1 on v0

v1 whole, which is shorter than its diff:
```python
import functools
import math

import jax
import jax.numpy as jnp
from jax import lax
from jax.experimental import pallas as pl
from jax.experimental.pallas import tpu as pltpu
from jax.sharding import PartitionSpec as P

HEAD_DIM = 128
MOST = 512
CHUNKS = 1
SCALE = HEAD_DIM ** (-0.5)
LOG2_SCALE = SCALE * math.log2(math.e)
HIDDEN = -1e30
AXES = ("ctx", "head")
NT = (((1,), (1,)), ((), ()))
NN = (((1,), (0,)), ((), ()))


def shift(value, steps):
    count = lax.axis_size(AXES)
    return lax.ppermute(value, AXES, [(i, i + steps) for i in range(count) if 0 <= i + steps < count])


def swap(value):
    return lax.ppermute(value, "head", [(i, i ^ 1) for i in range(lax.axis_size("head"))])


def dot(a, b, dims):
    return lax.dot_general(a, b, dims, preferred_element_type=jnp.float32)


def delta_kernel(g_ref, o_ref, delta_ref):
    for h in range(delta_ref.shape[0]):
        cols = slice(h * HEAD_DIM, (h + 1) * HEAD_DIM)
        prod = g_ref[:, cols].astype(jnp.float32) * o_ref[:, cols].astype(jnp.float32)
        delta_ref[h : h + 1, :] = jnp.sum(prod.T, axis=0, keepdims=True)


def row_delta(out_grad, attn_out):
    tok, width = out_grad.shape
    return pl.pallas_call(
        delta_kernel,
        out_shape=jax.ShapeDtypeStruct((width // HEAD_DIM, tok), jnp.float32),
        cost_estimate=pl.CostEstimate(flops=2 * tok * width, bytes_accessed=4 * tok * width, transcendentals=0),
        name="row_delta",
    )(out_grad, attn_out)


def attention_kernel(
    tok, group, kv_heads,
    q_ref, g_ref, delta_ref, own_ref, b1_ref, a1_ref, b2_ref, a2_ref,
    dq_ref, own_out, d1_out, d2_out, d3_out, d4_out,
    bias_scr, p_scr, ds_scr,
):
    pieces = (a2_ref, b2_ref, a1_ref, b1_ref, own_ref)
    outs = (d4_out, d3_out, d2_out, d1_out, own_out)

    def documents(ref):
        rows = ref[2 * tok : 2 * tok + 16, :tok].astype(jnp.float32)
        return jnp.concatenate([rows] * (tok // 16), axis=0)

    mine = documents(own_ref)
    for at, ref in enumerate(pieces):
        same = documents(ref).T == mine
        if ref is own_ref:
            key_at = lax.broadcasted_iota(jnp.int32, (tok, tok), 0)
            row_at = lax.broadcasted_iota(jnp.int32, (tok, tok), 1)
            same = same & (key_at <= row_at)
        bias_scr[at * tok : (at + 1) * tok, :] = jnp.where(same, 0.0, HIDDEN)

    def one_kv_head(j):
        cols = pl.ds(pl.multiple_of(j * HEAD_DIM, HEAD_DIM), HEAD_DIM)
        keys = jnp.concatenate([ref[:tok, cols] for ref in pieces], axis=0)
        values = jnp.concatenate([ref[tok : 2 * tok, cols] for ref in pieces], axis=0)
        keys_t = jnp.concatenate([ref[:tok, cols].T for ref in pieces], axis=1)

        def head_cols(h):
            return pl.ds(pl.multiple_of((j * group + h) * HEAD_DIM, HEAD_DIM), HEAD_DIM)

        bias = bias_scr[...]
        for pair in range(group // 2):
            q2 = jnp.concatenate([q_ref[:, head_cols(2 * pair + i)] for i in range(2)], axis=0)
            g2 = jnp.concatenate([g_ref[:, head_cols(2 * pair + i)] for i in range(2)], axis=0)
            d2 = jnp.concatenate([delta_ref[pl.ds(j * group + 2 * pair + i, 1), :] for i in range(2)], axis=1)
            s = dot(keys, q2, NT) + jnp.concatenate([bias, bias], axis=1)
            top = jnp.max(s, axis=0, keepdims=True)
            e = jnp.exp2((s - top) * LOG2_SCALE)
            prob = e * (1.0 / jnp.sum(e, axis=0, keepdims=True))
            dprob = dot(values, g2, NT)
            at = slice(2 * pair * tok, 2 * (pair + 1) * tok)
            p_scr[:, at] = prob.astype(jnp.bfloat16)
            ds_scr[:, at] = (prob * (dprob - d2)).astype(jnp.bfloat16)
        q_all = jnp.concatenate([q_ref[:, head_cols(h)] for h in range(group)], axis=0)
        g_all = jnp.concatenate([g_ref[:, head_cols(h)] for h in range(group)], axis=0)
        dk = dot(ds_scr[...], q_all, NN) * SCALE
        dv = dot(p_scr[...], g_all, NN)
        for at, out in enumerate(outs):
            out[:tok, cols] = dk[at * tok : (at + 1) * tok].astype(out.dtype)
            out[tok : 2 * tok, cols] = dv[at * tok : (at + 1) * tok].astype(out.dtype)
        dq_t = dot(keys_t, ds_scr[...], NN) * SCALE
        for h in range(group):
            dq_ref[:, head_cols(h)] = dq_t[:, h * tok : (h + 1) * tok].T.astype(jnp.bfloat16)

    lax.fori_loop(0, kv_heads, lambda j, c: (one_kv_head(j), c)[1], 0)


def attention(query, out_grad, delta, own, b1, a1, b2, a2, group, chunk, chunks):
    tok = query.shape[0]
    width = own.shape[1]
    kv_heads = width // HEAD_DIM
    wide = kv_heads * group * HEAD_DIM
    ext = MOST + tok
    whole = lambda a: pl.BlockSpec(a.shape, lambda i: (0, 0))
    pending = jax.ShapeDtypeStruct((2 * tok, width), jnp.bfloat16)
    out_shape = (
        jax.ShapeDtypeStruct((tok, wide), jnp.bfloat16),
        jax.ShapeDtypeStruct((2 * tok, width), jnp.float32),
        pending, pending, pending, pending,
    )
    return pl.pallas_call(
        functools.partial(attention_kernel, tok, group, kv_heads),
        grid=(1,),
        in_specs=[
            pl.BlockSpec((tok, wide), lambda i: (0, chunk)),
            pl.BlockSpec((tok, wide), lambda i: (0, chunk)),
            pl.BlockSpec((kv_heads * group, tok), lambda i: (chunk, 0)),
        ] + [whole(own)] * 5,
        out_specs=tuple(whole(o) for o in out_shape),
        out_shape=out_shape,
        scratch_shapes=[
            pltpu.VMEM((ext, tok), jnp.float32),
            pltpu.VMEM((ext, group * tok), jnp.bfloat16),
            pltpu.VMEM((ext, group * tok), jnp.bfloat16),
        ],
        compiler_params=pltpu.CompilerParams(vmem_limit_bytes=48 * 2**20),
        cost_estimate=pl.CostEstimate(
            flops=10 * ext * tok * kv_heads * group * HEAD_DIM,
            bytes_accessed=6 * tok * wide + 12 * ext * width,
            transcendentals=ext * tok * kv_heads * group,
        ),
        name="attention_backward",
    )(query, out_grad, delta, own, b1, a1, b2, a2)


def per_device(query, key, value, attn_out, out_grad, segments):
    tok = query.shape[0]
    heads = query.shape[1] // HEAD_DIM
    kv_heads = key.shape[1] // HEAD_DIM
    group = heads // kv_heads
    width = key.shape[1] // CHUNKS
    odd = lax.axis_index("head") % 2 == 1
    documents = jnp.tile((segments + 1).astype(jnp.bfloat16)[None, :], (16, width // tok))
    delta = row_delta(out_grad, attn_out)
    dq_parts, dk_parts, dv_parts = [], [], []
    for c in range(CHUNKS):
        cols = slice(c * width, (c + 1) * width)
        own = jnp.concatenate([key[:, cols], value[:, cols], documents], axis=0)
        a1 = shift(own, 2)
        a2 = shift(a1, 2)
        b1 = swap(jnp.where(odd, a1, own))
        b2 = swap(jnp.where(odd, a2, a1))
        dq, mine, d1, d2, d3, d4 = attention(query, out_grad, delta, own, b1, a1, b2, a2, group, c, CHUNKS)
        c3 = swap(d3)
        c1 = swap(d1)
        add = lambda *terms: sum(t.astype(jnp.float32) for t in terms)
        zero = jnp.zeros_like(c1)
        far = add(d4, jnp.where(odd, c3, zero)).astype(jnp.bfloat16)
        e1 = shift(far, -2)
        near = add(d2, jnp.where(odd, c1, c3), e1).astype(jnp.bfloat16)
        e2 = shift(near, -2)
        total = add(mine, jnp.where(odd, zero, c1), e2).astype(jnp.bfloat16)
        dq_parts.append(dq)
        dk_parts.append(total[:tok])
        dv_parts.append(total[tok:])
    join = lambda parts: parts[0] if len(parts) == 1 else jnp.concatenate(parts, axis=1)
    return join(dq_parts), join(dk_parts), join(dv_parts)


def solution(mesh):
    split = P(AXES, None)
    return jax.shard_map(
        per_device,
        mesh=mesh,
        in_specs=(split, split, split, split, split, P(AXES)),
        out_specs=(split, split, split),
        check_vma=False,
    )
```

time: 694 us -> 95.4 us (0.14)
  waiting for transfers between devices: 342 us -> 44.8 us
  blocking collectives: 98.9 us -> 0 us
  local copies, waits for them, and re-layouts: 85.5 us -> 1.47 us
  matrix products: 66.1 us -> 0 us
  starting transfers between devices: 70.4 us -> 30.3 us
  other arithmetic: 18.6 us -> 2.93 us
  Pallas kernels: 0 us -> 14.7 us
    all_to_all x8 -> x0, waiting for transfers between devices: 327 us -> none  [the longest x1 53.8 us: per_device(): lax.all_to_all(g3, 'head', split_axis=1, concat_axis=0, tiled=True)]
    all_gather x1 -> x0, blocking collectives: 98.9 us -> none  [per_device(): seg_own = lax.all_gather(segments, 'head', axis=0, tiled=True)]
    dot_general x40 -> x0, matrix products: 66.1 us -> none  [the longest x8 18.5 us: block_math(): jnp.einsum('hqk,qhd->khd', prob_low, g_blk, preferred_element_type=jnp.fl...]
    all_to_all x8 -> x0, starting transfers between devices: 58.2 us -> none  [the longest x1 16.5 us: per_device(): lax.all_to_all(k3, 'head', split_axis=1, concat_axis=0, tiled=True)]
    ppermute x5 -> x8, waiting for transfers between devices: 15.5 us -> 44.8 us  [the longest x4 37.3 us: shift(): lax.ppermute(value, AXES, [(i, i + steps) for i in range(count) if 0 <= i...]
    dynamic_update_slice x40 -> x0, local copies, waits for them, and re-layouts: 26 us -> none  [per_device(): lax.map(one_block, jnp.arange(nblocks, dtype=jnp.int32))]
    unnamed x33 -> x10, local copies, waits for them, and re-layouts: 26 us -> 0.74 us
    ppermute x5 -> x8, starting transfers between devices: 12.2 us -> 30.3 us  [the longest x4 18.5 us: shift(): lax.ppermute(value, AXES, [(i, i + steps) for i in range(count) if 0 <= i...]
  transfers between devices with their start and end apart: 13 -> 8, of which waited for: 11 -> 7; matrix products, arithmetic and copies ran while one was open for 6% -> 0% of each run, Pallas kernels for 0% -> 3%
where the time goes in v1:
time: 95.4 us; the launch traced here: 95 us
  waiting for transfers between devices  44.8 us (47%)
  starting transfers between devices  30.3 us (32%)
  Pallas kernels  14.7 us (15%)
  other arithmetic  2.93 us (3%)
  local copies, waits for them, and re-layouts  1.47 us (2%)
    ppermute x4, waiting for transfers between devices, shift(): lax.ppermute(value, AXES, [(i, i + steps) for i in range(count) if 0 <= i...  37.3 us
    ppermute x4, starting transfers between devices, shift(): lax.ppermute(value, AXES, [(i, i + steps) for i in range(count) if 0 <= i...  18.5 us
    pallas_call x1, Pallas kernels, attention(): pl.pallas_call(functools.partial(attention_kernel, tok, group, kv_heads),...  12 us
    ppermute x4, starting transfers between devices, swap(): lax.ppermute(value, 'head', [(i, i ^ 1) for i in range(lax.axis_size('hea...  11.8 us
    ppermute x4, waiting for transfers between devices, swap(): lax.ppermute(value, 'head', [(i, i ^ 1) for i in range(lax.axis_size('hea...  7.55 us
    pallas_call x1, Pallas kernels, row_delta(): pl.pallas_call(delta_kernel, out_shape=jax.ShapeDtypeStruct((width // HEA...  2.76 us
  transfers between devices with their start and end apart: 8, of which 7 were waited for; matrix products, arithmetic and copies ran while one was open for 0% of the time, Pallas kernels for 3%

profile of v1, /device:TPU:6, one launch (start us, length us, event | category | flops | bytes accessed | tf_op | source)
XLA Modules:
  0.0 95.0 jit_solution(5200422029253643931)
XLA Ops:
  0.6 0.7 add_convert_fusion.3
  1.3 0.0 copy-start.3
  1.3 0.0 copy-start.4
  1.3 1.0 %pad_maximum_fusion.own_ref = bf16[272,512]{1,0:T(8,128)(2,1)S(1)} fusion(bf16[16,512]{1,0:T(8,128)(2,1)S(1)} %tile.12, bf16[128,512]{1,0:T(8,128)(2,1)} %param.8, bf16[128,512]{1,0:T(8,128)(2,1)} %param.7), kind=kLoop, calls=%fused_computation.3 | loop fusion | flops 835584 | bytes 557056 | tf_op jit(solution)/shard_map/concatenate | solution.py:160
  2.4 3.8 %collective-permute-start = (bf16[272,512]{1,0:T(8,128)(2,1)S(1)}, bf16[272,512]{1,0:T(8,128)(2,1)S(1)}, u32[]{:S(2)}, u32[]{:S(2)}) collective-permute-start(bf16[272,512]{1,0:T(8,128)(2,1)S(1)} %pad_maximum_fusion.own_ref), channel_id=1, source_target_pairs={{0,2},{1,3},{2,4},{3,5},{4,6},{5,7},{6,8},{7,9},{8,10},{9,11},{10,... | collective-permute-start | bytes 835592 | tf_op jit(solution)/shard_map/ppermute | solution.py:24
  6.2 16.3 %collective-permute-done.a1_ref = bf16[272,512]{1,0:T(8,128)(2,1)S(1)} collective-permute-done((bf16[272,512]{1,0:T(8,128)(2,1)S(1)}, bf16[272,512]{1,0:T(8,128)(2,1)S(1)}, u32[]{:S(2)}, u32[]{:S(2)}) %collective-permute-start) | collective-permute-done | bytes 278560 | tf_op jit(solution)/shard_map/ppermute | solution.py:24
  22.5 1.9 %collective-permute-start.2 = (bf16[272,512]{1,0:T(8,128)(2,1)S(1)}, bf16[272,512]{1,0:T(8,128)(2,1)S(1)}, u32[]{:S(2)}, u32[]{:S(2)}) collective-permute-start(bf16[272,512]{1,0:T(8,128)(2,1)S(1)} %collective-permute-done.a1_ref), channel_id=1, source_target_pairs={{0,2},{1,3},{2,4},{3,5},{4,6},{5,7},{6,8},{7,9},{8,10},{9,11},{10,... | collective-permute-start | bytes 835592 | tf_op jit(solution)/shard_map/ppermute | solution.py:24
  24.4 11.0 %collective-permute-done.2.a2_ref = bf16[272,512]{1,0:T(8,128)(2,1)S(1)} collective-permute-done((bf16[272,512]{1,0:T(8,128)(2,1)S(1)}, bf16[272,512]{1,0:T(8,128)(2,1)S(1)}, u32[]{:S(2)}, u32[]{:S(2)}) %collective-permute-start.2) | collective-permute-done | bytes 278560 | tf_op jit(solution)/shard_map/ppermute | solution.py:24
  35.4 0.0 copy-done.3
  35.4 0.0 copy-done.4
  35.4 0.9 broadcast_select_fusion
  36.3 2.7 %collective-permute-start.3 = (bf16[272,512]{1,0:T(8,128)(2,1)}, bf16[272,512]{1,0:T(8,128)(2,1)S(1)}, u32[]{:S(2)}, u32[]{:S(2)}) collective-permute-start(bf16[272,512]{1,0:T(8,128)(2,1)} %get-tuple-element.15), channel_id=1, source_target_pairs={{0,1},{1,0},{2,3},{3,2},{4,5},{5,4},{6,7},{7,6},{8,9},{9,8},{10,11... | collective-permute-start | bytes 835592 | tf_op jit(solution)/shard_map/ppermute | solution.py:28
  39.0 0.0 copy-start
  39.0 0.0 copy-start.2
  39.0 3.3 %collective-permute-start.1 = (bf16[272,512]{1,0:T(8,128)(2,1)}, bf16[272,512]{1,0:T(8,128)(2,1)S(1)}, u32[]{:S(2)}, u32[]{:S(2)}) collective-permute-start(bf16[272,512]{1,0:T(8,128)(2,1)} %get-tuple-element.16), channel_id=1, source_target_pairs={{0,1},{1,0},{2,3},{3,2},{4,5},{5,4},{6,7},{7,6},{8,9},{9,8},{10,11... | collective-permute-start | bytes 835592 | tf_op jit(solution)/shard_map/ppermute | solution.py:28
  42.3 2.8 %row_delta.1.delta_ref = f32[32,128]{1,0:T(8,128)} custom-call(bf16[128,4096]{1,0:T(8,128)(2,1)} %g_ref.3, bf16[128,4096]{1,0:T(8,128)(2,1)} %o_ref.1), custom_call_target="tpu_custom_call" | custom-call | flops 1048576 | bytes 2097152 | tf_op jit(solution)/shard_map/row_delta/pallas_call | solution.py:44
  45.0 1.5 %collective-permute-done.3.b2_ref = bf16[272,512]{1,0:T(8,128)(2,1)S(1)} collective-permute-done((bf16[272,512]{1,0:T(8,128)(2,1)}, bf16[272,512]{1,0:T(8,128)(2,1)S(1)}, u32[]{:S(2)}, u32[]{:S(2)}) %collective-permute-start.3) | collective-permute-done | bytes 278560 | tf_op jit(solution)/shard_map/ppermute | solution.py:28
  46.5 3.0 %collective-permute-done.1.b1_ref = bf16[272,512]{1,0:T(8,128)(2,1)S(1)} collective-permute-done((bf16[272,512]{1,0:T(8,128)(2,1)}, bf16[272,512]{1,0:T(8,128)(2,1)S(1)}, u32[]{:S(2)}, u32[]{:S(2)}) %collective-permute-start.1) | collective-permute-done | bytes 278560 | tf_op jit(solution)/shard_map/ppermute | solution.py:28
  49.5 0.0 copy-done
  49.5 0.0 copy-done.2
  49.5 0.0 copy-start.1
  49.5 0.7 copy-done.1
  50.2 12.0 %attention_backward.1 = (bf16[128,4096]{1,0:T(8,128)(2,1)}, f32[256,512]{1,0:T(8,128)S(1)}, bf16[256,512]{1,0:T(8,128)(2,1)S(1)}, bf16[256,512]{1,0:T(8,128)(2,1...) custom-call(bf16[128,4096]{1,0:T(8,128)(2,1)S(1)} %copy-done.2, bf16[128,4096]{1,0:T(8,128)(2,1)S(1)} %copy-done, ...), custom_call_target="tpu_custom_call" | custom-call | flops 3355443200 | bytes 7077888 | tf_op jit(solution)/shard_map/attention_backward/pallas_call | solution.py:123
  62.2 3.1 %collective-permute-start.5 = (bf16[256,512]{1,0:T(8,128)(2,1)S(1)}, bf16[256,512]{1,0:T(8,128)(2,1)S(1)}, u32[]{:S(2)}, u32[]{:S(2)}) collective-permute-start(bf16[256,512]{1,0:T(8,128)(2,1)S(1)} %get-tuple-element.13), channel_id=1, source_target_pairs={{0,1},{1,0},{2,3},{3,2},{4,5},{5,4},{6,7},{7,6},{8,9},{9,8},{10,11... | collective-permute-start | bytes 786440 | tf_op jit(solution)/shard_map/ppermute | solution.py:28
  65.3 2.8 %collective-permute-start.4 = (bf16[256,512]{1,0:T(8,128)(2,1)S(1)}, bf16[256,512]{1,0:T(8,128)(2,1)S(1)}, u32[]{:S(2)}, u32[]{:S(2)}) collective-permute-start(bf16[256,512]{1,0:T(8,128)(2,1)S(1)} %get-tuple-element.11), channel_id=1, source_target_pairs={{0,1},{1,0},{2,3},{3,2},{4,5},{5,4},{6,7},{7,6},{8,9},{9,8},{10,11... | collective-permute-start | bytes 786440 | tf_op jit(solution)/shard_map/ppermute | solution.py:28
  68.0 3.1 %collective-permute-done.5 = bf16[256,512]{1,0:T(8,128)(2,1)S(1)} collective-permute-done((bf16[256,512]{1,0:T(8,128)(2,1)S(1)}, bf16[256,512]{1,0:T(8,128)(2,1)S(1)}, u32[]{:S(2)}, u32[]{:S(2)}) %collective-permute-start.5) | collective-permute-done | bytes 262176 | tf_op jit(solution)/shard_map/ppermute | solution.py:28
  71.1 0.1 add_convert_fusion.2
  71.2 4.4 %collective-permute-start.6 = (bf16[256,512]{1,0:T(8,128)(2,1)S(1)}, bf16[256,512]{1,0:T(8,128)(2,1)S(1)}, u32[]{:S(2)}, u32[]{:S(2)}) collective-permute-start(bf16[256,512]{1,0:T(8,128)(2,1)S(1)} %add_convert_fusion.2), channel_id=1, source_target_pairs={{2,0},{3,1},{4,2},{5,3},{6,4},{7,5},{8,6},{9,7},{10,8},{11,9},{12,... | collective-permute-start | bytes 786440 | tf_op jit(solution)/shard_map/ppermute | solution.py:24
  75.6 0.0 collective-permute-done.4
  75.7 6.2 %collective-permute-done.6 = bf16[256,512]{1,0:T(8,128)(2,1)S(1)} collective-permute-done((bf16[256,512]{1,0:T(8,128)(2,1)S(1)}, bf16[256,512]{1,0:T(8,128)(2,1)S(1)}, u32[]{:S(2)}, u32[]{:S(2)}) %collective-permute-start.6) | collective-permute-done | bytes 262176 | tf_op jit(solution)/shard_map/ppermute | solution.py:24
  81.8 0.1 add_convert_fusion.1
  81.9 8.3 %collective-permute-start.7 = (bf16[256,512]{1,0:T(8,128)(2,1)S(1)}, bf16[256,512]{1,0:T(8,128)(2,1)S(1)}, u32[]{:S(2)}, u32[]{:S(2)}) collective-permute-start(bf16[256,512]{1,0:T(8,128)(2,1)S(1)} %add_convert_fusion.1), channel_id=1, source_target_pairs={{2,0},{3,1},{4,2},{5,3},{6,4},{7,5},{8,6},{9,7},{10,8},{11,9},{12,... | collective-permute-start | bytes 786440 | tf_op jit(solution)/shard_map/ppermute | solution.py:24
  90.3 3.9 %collective-permute-done.7 = bf16[256,512]{1,0:T(8,128)(2,1)S(1)} collective-permute-done((bf16[256,512]{1,0:T(8,128)(2,1)S(1)}, bf16[256,512]{1,0:T(8,128)(2,1)S(1)}, u32[]{:S(2)}, u32[]{:S(2)}) %collective-permute-start.7) | collective-permute-done | bytes 262176 | tf_op jit(solution)/shard_map/ppermute | solution.py:24
  94.2 0.1 add_convert_fusion
  94.3 0.7 fusion
  (2 shorter events, 0.0 us)
Async XLA Ops:
  1.3 34.0 %copy-start.3 = (bf16[128,512]{1,0:T(8,128)(2,1)S(1)}, bf16[128,512]{1,0:T(8,128)(2,1)}, u32[]{:S(2)}) copy-start(bf16[128,512]{1,0:T(8,128)(2,1)} %param.8) | copy-start | bytes 393220
  1.3 34.0 %copy-start.4 = (bf16[128,512]{1,0:T(8,128)(2,1)S(1)}, bf16[128,512]{1,0:T(8,128)(2,1)}, u32[]{:S(2)}) copy-start(bf16[128,512]{1,0:T(8,128)(2,1)} %param.7) | copy-start | bytes 393220
  2.4 20.1 %collective-permute-start = (bf16[272,512]{1,0:T(8,128)(2,1)S(1)}, bf16[272,512]{1,0:T(8,128)(2,1)S(1)}, u32[]{:S(2)}, u32[]{:S(2)}) collective-permute-start(bf16[272,512]{1,0:T(8,128)(2,1)S(1)} %pad_maximum_fusion.own_ref), channel_id=1, source_target_pairs={{0,2},{1,3},{2,4},{3,5},{4,6},{5,7},{6,8},{7,9},{8,10},{9,11},{10,... | collective-permute-start | bytes 835592 | tf_op jit(solution)/shard_map/ppermute | solution.py:24
  22.5 12.9 %collective-permute-start.2 = (bf16[272,512]{1,0:T(8,128)(2,1)S(1)}, bf16[272,512]{1,0:T(8,128)(2,1)S(1)}, u32[]{:S(2)}, u32[]{:S(2)}) collective-permute-start(bf16[272,512]{1,0:T(8,128)(2,1)S(1)} %collective-permute-done.a1_ref), channel_id=1, source_target_pairs={{0,2},{1,3},{2,4},{3,5},{4,6},{5,7},{6,8},{7,9},{8,10},{9,11},{10,... | collective-permute-start | bytes 835592 | tf_op jit(solution)/shard_map/ppermute | solution.py:24
  36.3 10.2 %collective-permute-start.3 = (bf16[272,512]{1,0:T(8,128)(2,1)}, bf16[272,512]{1,0:T(8,128)(2,1)S(1)}, u32[]{:S(2)}, u32[]{:S(2)}) collective-permute-start(bf16[272,512]{1,0:T(8,128)(2,1)} %get-tuple-element.15), channel_id=1, source_target_pairs={{0,1},{1,0},{2,3},{3,2},{4,5},{5,4},{6,7},{7,6},{8,9},{9,8},{10,11... | collective-permute-start | bytes 835592 | tf_op jit(solution)/shard_map/ppermute | solution.py:28
  39.0 10.5 %copy-start = (bf16[128,4096]{1,0:T(8,128)(2,1)S(1)}, bf16[128,4096]{1,0:T(8,128)(2,1)}, u32[]{:S(2)}) copy-start(bf16[128,4096]{1,0:T(8,128)(2,1)} %g_ref.3) | copy-start | bytes 3145732
  39.0 10.5 %copy-start.2 = (bf16[128,4096]{1,0:T(8,128)(2,1)S(1)}, bf16[128,4096]{1,0:T(8,128)(2,1)}, u32[]{:S(2)}) copy-start(bf16[128,4096]{1,0:T(8,128)(2,1)} %q_ref.1) | copy-start | bytes 3145732
  39.0 10.5 %collective-permute-start.1 = (bf16[272,512]{1,0:T(8,128)(2,1)}, bf16[272,512]{1,0:T(8,128)(2,1)S(1)}, u32[]{:S(2)}, u32[]{:S(2)}) collective-permute-start(bf16[272,512]{1,0:T(8,128)(2,1)} %get-tuple-element.16), channel_id=1, source_target_pairs={{0,1},{1,0},{2,3},{3,2},{4,5},{5,4},{6,7},{7,6},{8,9},{9,8},{10,11... | collective-permute-start | bytes 835592 | tf_op jit(solution)/shard_map/ppermute | solution.py:28
  49.5 0.7 copy-start.1
  62.2 9.0 %collective-permute-start.5 = (bf16[256,512]{1,0:T(8,128)(2,1)S(1)}, bf16[256,512]{1,0:T(8,128)(2,1)S(1)}, u32[]{:S(2)}, u32[]{:S(2)}) collective-permute-start(bf16[256,512]{1,0:T(8,128)(2,1)S(1)} %get-tuple-element.13), channel_id=1, source_target_pairs={{0,1},{1,0},{2,3},{3,2},{4,5},{5,4},{6,7},{7,6},{8,9},{9,8},{10,11... | collective-permute-start | bytes 786440 | tf_op jit(solution)/shard_map/ppermute | solution.py:28
  65.3 10.4 %collective-permute-start.4 = (bf16[256,512]{1,0:T(8,128)(2,1)S(1)}, bf16[256,512]{1,0:T(8,128)(2,1)S(1)}, u32[]{:S(2)}, u32[]{:S(2)}) collective-permute-start(bf16[256,512]{1,0:T(8,128)(2,1)S(1)} %get-tuple-element.11), channel_id=1, source_target_pairs={{0,1},{1,0},{2,3},{3,2},{4,5},{5,4},{6,7},{7,6},{8,9},{9,8},{10,11... | collective-permute-start | bytes 786440 | tf_op jit(solution)/shard_map/ppermute | solution.py:28
  71.2 10.6 %collective-permute-start.6 = (bf16[256,512]{1,0:T(8,128)(2,1)S(1)}, bf16[256,512]{1,0:T(8,128)(2,1)S(1)}, u32[]{:S(2)}, u32[]{:S(2)}) collective-permute-start(bf16[256,512]{1,0:T(8,128)(2,1)S(1)} %add_convert_fusion.2), channel_id=1, source_target_pairs={{2,0},{3,1},{4,2},{5,3},{6,4},{7,5},{8,6},{9,7},{10,8},{11,9},{12,... | collective-permute-start | bytes 786440 | tf_op jit(solution)/shard_map/ppermute | solution.py:24
  81.9 12.2 %collective-permute-start.7 = (bf16[256,512]{1,0:T(8,128)(2,1)S(1)}, bf16[256,512]{1,0:T(8,128)(2,1)S(1)}, u32[]{:S(2)}, u32[]{:S(2)}) collective-permute-start(bf16[256,512]{1,0:T(8,128)(2,1)S(1)} %add_convert_fusion.1), channel_id=1, source_target_pairs={{2,0},{3,1},{4,2},{5,3},{6,4},{7,5},{8,6},{9,7},{10,8},{11,9},{12,... | collective-permute-start | bytes 786440 | tf_op jit(solution)/shard_map/ppermute | solution.py:24

commit v2 on v1

v2 whole, which is shorter than its diff:
```python
import functools
import math

import jax
import jax.numpy as jnp
from jax import lax
from jax.experimental import pallas as pl
from jax.experimental.pallas import tpu as pltpu
from jax.sharding import PartitionSpec as P

HEAD_DIM = 128
MOST = 512
LOG2_SCALE = HEAD_DIM ** (-0.5) * math.log2(math.e)
SCALE = HEAD_DIM ** (-0.5)
HIDDEN = -1e30
AXES = ("ctx", "head")
NT = (((1,), (1,)), ((), ()))
NN = (((1,), (0,)), ((), ()))


def shift(value, steps):
    count = lax.axis_size(AXES)
    return lax.ppermute(value, AXES, [(i, i + steps) for i in range(count) if 0 <= i + steps < count])


def dot(a, b, dims):
    return lax.dot_general(a, b, dims, preferred_element_type=jnp.float32)


def head_cols(h):
    return pl.ds(pl.multiple_of(h * HEAD_DIM, HEAD_DIM), HEAD_DIM)


def fill_bias(bias_scr, own_ref, pieces, tok):
    def documents(ref):
        rows = ref[2 * tok : 2 * tok + 16, :tok].astype(jnp.float32)
        return jnp.concatenate([rows] * (tok // 16), axis=0)

    mine = documents(own_ref)
    for at, ref in enumerate(pieces):
        same = documents(ref).T == mine
        if ref is own_ref:
            key_at = lax.broadcasted_iota(jnp.int32, (tok, tok), 0)
            row_at = lax.broadcasted_iota(jnp.int32, (tok, tok), 1)
            same = same & (key_at <= row_at)
        bias_scr[at * tok : (at + 1) * tok, :] = jnp.where(same, 0.0, HIDDEN)


def stack(pieces, rows, cols):
    return jnp.concatenate([ref[rows, cols] for ref in pieces], axis=0)


def pair_rows(ref, first):
    return jnp.concatenate([ref[:, head_cols(first + i)] for i in range(2)], axis=0)


def pair_stat(ref, first):
    return jnp.concatenate([ref[pl.ds(first + i, 1), :] for i in range(2)], axis=1)


def put_stat(ref, first, value):
    tok = ref.shape[1]
    for i in range(2):
        ref[pl.ds(first + i, 1), :] = value[:, i * tok : (i + 1) * tok]


def near_stats_kernel(tok, group, kv_heads, q_ref, g_ref, o_ref, own_ref, r1_ref, r2_ref, top_ref, sum_ref, delta_ref, bias_scr):
    pieces = (r2_ref, r1_ref, own_ref)
    fill_bias(bias_scr, own_ref, pieces, tok)

    def one_kv_head(j, carry):
        keys = stack(pieces, slice(0, tok), head_cols(j))
        for pair in range(group // 2):
            first = j * group + 2 * pair
            bias = bias_scr[...]
            s = dot(keys, pair_rows(q_ref, first), NT) + jnp.concatenate([bias, bias], axis=1)
            top = jnp.max(s, axis=0, keepdims=True)
            put_stat(top_ref, first, top)
            put_stat(sum_ref, first, jnp.sum(jnp.exp2((s - top) * LOG2_SCALE), axis=0, keepdims=True))
            prod = pair_rows(g_ref, first).astype(jnp.float32) * pair_rows(o_ref, first).astype(jnp.float32)
            put_stat(delta_ref, first, jnp.sum(prod.T, axis=0, keepdims=True))
        return carry

    lax.fori_loop(0, kv_heads, one_kv_head, 0)


def gradients(ds, p, q_ref, g_ref, j, group):
    q_all = jnp.concatenate([q_ref[:, head_cols(j * group + h)] for h in range(group)], axis=0)
    g_all = jnp.concatenate([g_ref[:, head_cols(j * group + h)] for h in range(group)], axis=0)
    return dot(ds, q_all, NN) * SCALE, dot(p, g_all, NN)


def put_gradients(outs, dk, dv, j, tok):
    for at, out in enumerate(outs):
        out[:tok, head_cols(j)] = dk[at * tok : (at + 1) * tok].astype(out.dtype)
        out[tok : 2 * tok, head_cols(j)] = dv[at * tok : (at + 1) * tok].astype(out.dtype)


def far_kernel(
    tok, group, kv_heads,
    q_ref, g_ref, own_ref, r3_ref, r4_ref, near_top_ref, near_sum_ref, delta_ref,
    d3_ref, d4_ref, top_ref, inv_ref, ds_ref,
    bias_scr, p_scr,
):
    pieces = (r4_ref, r3_ref)
    fill_bias(bias_scr, own_ref, pieces, tok)

    def one_kv_head(j, carry):
        keys = stack(pieces, slice(0, tok), head_cols(j))
        values = stack(pieces, slice(tok, 2 * tok), head_cols(j))
        for pair in range(group // 2):
            first = j * group + 2 * pair
            bias = bias_scr[...]
            s = dot(keys, pair_rows(q_ref, first), NT) + jnp.concatenate([bias, bias], axis=1)
            near_top = pair_stat(near_top_ref, first)
            top = jnp.maximum(near_top, jnp.max(s, axis=0, keepdims=True))
            e = jnp.exp2((s - top) * LOG2_SCALE)
            total = pair_stat(near_sum_ref, first) * jnp.exp2((near_top - top) * LOG2_SCALE) + jnp.sum(e, axis=0, keepdims=True)
            inv = 1.0 / total
            put_stat(top_ref, first, top)
            put_stat(inv_ref, first, inv)
            prob = e * inv
            dprob = dot(values, pair_rows(g_ref, first), NT)
            p_scr[:, 2 * pair * tok : 2 * (pair + 1) * tok] = prob.astype(jnp.bfloat16)
            low = (prob * (dprob - pair_stat(delta_ref, first))).astype(jnp.bfloat16)
            for i in range(2):
                ds_ref[:, head_cols(first + i)] = low[:, i * tok : (i + 1) * tok]
        cols = pl.ds(pl.multiple_of(j * group * HEAD_DIM, HEAD_DIM), group * HEAD_DIM)
        dk, dv = gradients(ds_ref[:, cols], p_scr[...], q_ref, g_ref, j, group)
        put_gradients((d4_ref, d3_ref), dk, dv, j, tok)
        return carry

    lax.fori_loop(0, kv_heads, one_kv_head, 0)


def near_kernel(
    tok, group, kv_heads,
    q_ref, g_ref, own_ref, r1_ref, r2_ref, r3_ref, r4_ref, top_ref, inv_ref, delta_ref, far_ds_ref,
    dq_ref, own_out, d1_ref, d2_ref,
    bias_scr, p_scr, ds_scr,
):
    pieces = (r2_ref, r1_ref, own_ref)
    fill_bias(bias_scr, own_ref, pieces, tok)

    def one_kv_head(j, carry):
        keys = stack(pieces, slice(0, tok), head_cols(j))
        values = stack(pieces, slice(tok, 2 * tok), head_cols(j))
        every = (r4_ref, r3_ref) + pieces
        keys_t = jnp.concatenate([ref[:tok, head_cols(j)].T for ref in every], axis=1)
        for pair in range(group // 2):
            first = j * group + 2 * pair
            bias = bias_scr[...]
            s = dot(keys, pair_rows(q_ref, first), NT) + jnp.concatenate([bias, bias], axis=1)
            prob = jnp.exp2((s - pair_stat(top_ref, first)) * LOG2_SCALE) * pair_stat(inv_ref, first)
            dprob = dot(values, pair_rows(g_ref, first), NT)
            at = slice(2 * pair * tok, 2 * (pair + 1) * tok)
            p_scr[:, at] = prob.astype(jnp.bfloat16)
            ds_scr[:, at] = (prob * (dprob - pair_stat(delta_ref, first))).astype(jnp.bfloat16)
        dk, dv = gradients(ds_scr[...], p_scr[...], q_ref, g_ref, j, group)
        put_gradients((d2_ref, d1_ref, own_out), dk, dv, j, tok)
        cols = pl.ds(pl.multiple_of(j * group * HEAD_DIM, HEAD_DIM), group * HEAD_DIM)
        ds_all = jnp.concatenate([far_ds_ref[:, cols], ds_scr[...]], axis=0)
        dq_t = dot(keys_t, ds_all, NN) * SCALE
        for h in range(group):
            dq_ref[:, head_cols(j * group + h)] = dq_t[:, h * tok : (h + 1) * tok].T.astype(jnp.bfloat16)
        return carry

    lax.fori_loop(0, kv_heads, one_kv_head, 0)


def call(kernel, name, args, out_shape, scratch, keys, products, sizes):
    tok, group, kv_heads = sizes
    whole = pl.BlockSpec(memory_space=pltpu.VMEM)
    pairs = keys * tok * group * kv_heads
    return pl.pallas_call(
        functools.partial(kernel, *sizes),
        in_specs=[whole] * len(args),
        out_specs=tuple(whole for _ in out_shape),
        out_shape=tuple(jax.ShapeDtypeStruct(s, d) for s, d in out_shape),
        scratch_shapes=[pltpu.VMEM(s, d) for s, d in scratch],
        compiler_params=pltpu.CompilerParams(vmem_limit_bytes=40 * 2**20),
        cost_estimate=pl.CostEstimate(
            flops=2 * products * pairs * HEAD_DIM, bytes_accessed=sum(a.size * a.dtype.itemsize for a in args), transcendentals=pairs
        ),
        name=name,
    )(*args)


def per_device(query, key, value, attn_out, out_grad, segments):
    tok = query.shape[0]
    heads = query.shape[1] // HEAD_DIM
    width = key.shape[1]
    kv_heads = width // HEAD_DIM
    group = heads // kv_heads
    sizes = (tok, group, kv_heads)
    f32, bf16 = jnp.float32, jnp.bfloat16
    documents = jnp.tile((segments + 1).astype(bf16)[None, :], (16, width // tok))
    own = jnp.concatenate([key, value, documents], axis=0)
    r2 = shift(own, 2)
    r1 = shift(own, 1)
    r4 = shift(r2, 2)
    r3 = shift(r1, 2)
    stat = ((heads, tok), f32)
    pending = ((2 * tok, width), bf16)
    near, far = 3 * tok, 2 * tok
    near_top, near_sum, delta = call(
        near_stats_kernel, "near_stats", (query, out_grad, attn_out, own, r1, r2),
        (stat, stat, stat), (((near, tok), f32),), near, 1, sizes,
    )
    d3, d4, top, inv, far_ds = call(
        far_kernel, "far_gradients", (query, out_grad, own, r3, r4, near_top, near_sum, delta),
        (pending, pending, stat, stat, ((far, heads * tok), bf16)),
        (((far, tok), f32), ((far, group * tok), bf16)), far, 4, sizes,
    )
    x4 = shift(d4, -2)
    x3 = shift(d3, -2)
    query_grad, mine, d1, d2 = call(
        near_kernel, "near_gradients", (query, out_grad, own, r1, r2, r3, r4, top, inv, delta, far_ds),
        (((tok, heads * HEAD_DIM), bf16), ((2 * tok, width), f32), pending, pending),
        (((near, tok), f32), ((near, group * tok), bf16), ((near, group * tok), bf16)), near, 5, sizes,
    )
    y2 = shift((d2.astype(f32) + x4.astype(f32)).astype(bf16), -2)
    y1 = shift((d1.astype(f32) + x3.astype(f32)).astype(bf16), -1)
    total = (mine + y2.astype(f32) + y1.astype(f32)).astype(bf16)
    return query_grad, total[:tok], total[tok:]


def solution(mesh):
    split = P(AXES, None)
    return jax.shard_map(
        per_device,
        mesh=mesh,
        in_specs=(split, split, split, split, split, P(AXES)),
        out_specs=(split, split, split),
        check_vma=False,
    )
```

time: 95.4 us -> 74.8 us (0.78)
  waiting for transfers between devices: 44.8 us -> 28 us
  starting transfers between devices: 30.3 us -> 24.9 us
  local copies, waits for them, and re-layouts: 1.47 us -> 4.4 us
  other arithmetic: 2.93 us -> 1.88 us
    ppermute x4 -> x0, starting transfers between devices: 11.8 us -> none  [swap(): lax.ppermute(value, 'head', [(i, i ^ 1) for i in range(lax.axis_size('hea...]
    ppermute x4 -> x8, waiting for transfers between devices: 37.3 us -> 28 us  [shift(): lax.ppermute(value, AXES, [(i, i + steps) for i in range(count) if 0 <= i...]
    ppermute x4 -> x0, waiting for transfers between devices: 7.55 us -> none  [swap(): lax.ppermute(value, 'head', [(i, i ^ 1) for i in range(lax.axis_size('hea...]
    ppermute x4 -> x8, starting transfers between devices: 18.5 us -> 24.9 us  [shift(): lax.ppermute(value, AXES, [(i, i + steps) for i in range(count) if 0 <= i...]
    unnamed x10 -> x6, local copies, waits for them, and re-layouts: 0.74 us -> 3.67 us
    pallas_call x2 -> x3, Pallas kernels: 14.7 us -> 14.5 us  [call(): pl.pallas_call(functools.partial(kernel, *sizes), in_specs=[whole] * len(...]
  transfers between devices with their start and end apart: 8 -> 8, of which waited for: 7 -> 5; matrix products, arithmetic and copies ran while one was open for 0% -> 0% of each run, Pallas kernels for 3% -> 13%
where the time goes in v2:
time: 74.8 us; the launch traced here: 74.3 us
  waiting for transfers between devices  28 us (37%)
  starting transfers between devices  24.9 us (33%)
  Pallas kernels  14.5 us (19%)
  local copies, waits for them, and re-layouts  4.4 us (6%)
  other arithmetic  1.88 us (3%)
  between operations  0.75 us (1%)
    ppermute x8, waiting for transfers between devices, shift(): lax.ppermute(value, AXES, [(i, i + steps) for i in range(count) if 0 <= i...  28 us
    ppermute x8, starting transfers between devices, shift(): lax.ppermute(value, AXES, [(i, i + steps) for i in range(count) if 0 <= i...  24.9 us
    pallas_call x3, Pallas kernels, call(): pl.pallas_call(functools.partial(kernel, *sizes), in_specs=[whole] * len(...  14.5 us
    unnamed x6, local copies, waits for them, and re-layouts  3.67 us
  transfers between devices with their start and end apart: 8, of which 5 were waited for; matrix products, arithmetic and copies ran while one was open for 0% of the time, Pallas kernels for 13%

profile of v2, /device:TPU:6, one launch (start us, length us, event | category | flops | bytes accessed | tf_op | source)
XLA Modules:
  0.0 74.3 jit_solution(3033788508215069913)
XLA Ops:
  0.6 0.7 add_convert_fusion.3
  1.3 1.0 %pad_maximum_fusion.own_ref = bf16[272,512]{1,0:T(8,128)(2,1)S(1)} fusion(bf16[16,512]{1,0:T(8,128)(2,1)S(1)} %tile.12, bf16[128,512]{1,0:T(8,128)(2,1)} %param.8, bf16[128,512]{1,0:T(8,128)(2,1)} %param.7), kind=kLoop, calls=%fused_computation.3 | loop fusion | flops 835584 | bytes 557056 | tf_op jit(solution)/shard_map/concatenate | solution.py:198
  2.3 3.8 %collective-permute-start.1 = (bf16[272,512]{1,0:T(8,128)(2,1)S(1)}, bf16[272,512]{1,0:T(8,128)(2,1)S(1)}, u32[]{:S(2)}, u32[]{:S(2)}) collective-permute-start(bf16[272,512]{1,0:T(8,128)(2,1)S(1)} %pad_maximum_fusion.own_ref), channel_id=1, source_target_pairs={{0,2},{1,3},{2,4},{3,5},{4,6},{5,7},{6,8},{7,9},{8,10},{9,11},{10,... | collective-permute-start | bytes 835592 | tf_op jit(solution)/shard_map/ppermute | solution.py:23
  6.1 3.5 %collective-permute-start = (bf16[272,512]{1,0:T(8,128)(2,1)S(1)}, bf16[272,512]{1,0:T(8,128)(2,1)S(1)}, u32[]{:S(2)}, u32[]{:S(2)}) collective-permute-start(bf16[272,512]{1,0:T(8,128)(2,1)S(1)} %pad_maximum_fusion.own_ref), channel_id=1, source_target_pairs={{0,1},{1,2},{2,3},{3,4},{4,5},{5,6},{6,7},{7,8},{8,9},{9,10},{10,1... | collective-permute-start | bytes 835592 | tf_op jit(solution)/shard_map/ppermute | solution.py:23
  9.6 12.8 %collective-permute-done.1.r2_ref = bf16[272,512]{1,0:T(8,128)(2,1)S(1)} collective-permute-done((bf16[272,512]{1,0:T(8,128)(2,1)S(1)}, bf16[272,512]{1,0:T(8,128)(2,1)S(1)}, u32[]{:S(2)}, u32[]{:S(2)}) %collective-permute-start.1) | collective-permute-done | bytes 278560 | tf_op jit(solution)/shard_map/ppermute | solution.py:23
  22.4 1.9 %collective-permute-start.3 = (bf16[272,512]{1,0:T(8,128)(2,1)S(1)}, bf16[272,512]{1,0:T(8,128)(2,1)S(1)}, u32[]{:S(2)}, u32[]{:S(2)}) collective-permute-start(bf16[272,512]{1,0:T(8,128)(2,1)S(1)} %collective-permute-done.1.r2_ref), channel_id=1, source_target_pairs={{0,2},{1,3},{2,4},{3,5},{4,6},{5,7},{6,8},{7,9},{8,10},{9,11},{10,... | collective-permute-start | bytes 835592 | tf_op jit(solution)/shard_map/ppermute | solution.py:23
  24.3 3.9 %collective-permute-done.r1_ref = bf16[272,512]{1,0:T(8,128)(2,1)S(1)} collective-permute-done((bf16[272,512]{1,0:T(8,128)(2,1)S(1)}, bf16[272,512]{1,0:T(8,128)(2,1)S(1)}, u32[]{:S(2)}, u32[]{:S(2)}) %collective-permute-start) | collective-permute-done | bytes 278560 | tf_op jit(solution)/shard_map/ppermute | solution.py:23
  28.2 1.9 %collective-permute-start.2 = (bf16[272,512]{1,0:T(8,128)(2,1)S(1)}, bf16[272,512]{1,0:T(8,128)(2,1)S(1)}, u32[]{:S(2)}, u32[]{:S(2)}) collective-permute-start(bf16[272,512]{1,0:T(8,128)(2,1)S(1)} %collective-permute-done.r1_ref), channel_id=1, source_target_pairs={{0,2},{1,3},{2,4},{3,5},{4,6},{5,7},{6,8},{7,9},{8,10},{9,11},{10,... | collective-permute-start | bytes 835592 | tf_op jit(solution)/shard_map/ppermute | solution.py:23
  30.1 0.0 copy-start
  30.1 1.2 %copy-done = bf16[128,4096]{1,0:T(8,128)(2,1)S(1)} copy-done((bf16[128,4096]{1,0:T(8,128)(2,1)S(1)}, bf16[128,4096]{1,0:T(8,128)(2,1)}, u32[]{:S(2)}) %copy-start) | copy-done | bytes 1048600
  31.3 0.0 copy-start.1
  31.3 1.2 %copy-done.1 = bf16[128,4096]{1,0:T(8,128)(2,1)S(1)} copy-done((bf16[128,4096]{1,0:T(8,128)(2,1)S(1)}, bf16[128,4096]{1,0:T(8,128)(2,1)}, u32[]{:S(2)}) %copy-start.1) | copy-done | bytes 1048600
  32.6 0.0 copy-start.2
  32.6 1.2 %copy-done.2 = bf16[128,4096]{1,0:T(8,128)(2,1)S(1)} copy-done((bf16[128,4096]{1,0:T(8,128)(2,1)S(1)}, bf16[128,4096]{1,0:T(8,128)(2,1)}, u32[]{:S(2)}) %copy-start.2) | copy-done | bytes 1048600
  33.8 2.9 %near_stats.1 = (f32[32,128]{1,0:T(8,128)S(1)}, f32[32,128]{1,0:T(8,128)S(1)}, f32[32,128]{1,0:T(8,128)S(1)}) custom-call(bf16[128,4096]{1,0:T(8,128)(2,1)S(1)} %copy-done.1, bf16[128,4096]{1,0:T(8,128)(2,1)S(1)} %copy-done.2, bf16[128,4096]{1,0:T(8,128)(2,1)S(1)} %copy-done, bf16[272,512]{1,0:T(8,128)(2,1)S(1)} %pad_maximum_fusion.own_ref, ...), custom_call_target="tpu_custom_call" | custom-call | flops 402653184 | bytes 3981312 | tf_op jit(solution)/shard_map/near_stats/pallas_call | solution.py:175
  36.7 0.0 collective-permute-done.3.r4_ref
  36.7 5.5 %collective-permute-done.2.r3_ref = bf16[272,512]{1,0:T(8,128)(2,1)S(1)} collective-permute-done((bf16[272,512]{1,0:T(8,128)(2,1)S(1)}, bf16[272,512]{1,0:T(8,128)(2,1)S(1)}, u32[]{:S(2)}, u32[]{:S(2)}) %collective-permute-start.2) | collective-permute-done | bytes 278560 | tf_op jit(solution)/shard_map/ppermute | solution.py:23
  42.2 4.9 %far_gradients.1 = (bf16[256,512]{1,0:T(8,128)(2,1)S(1)}, bf16[256,512]{1,0:T(8,128)(2,1)S(1)}, f32[32,128]{1,0:T(8,128)S(1)}, f32[32,128]{1,0:T(8,128)S(1)}, bf16[256,4096]{1,0:T(8,128)(2,1)S(1)}) custom-call(bf16[128,4096]{1,0:T(8,128)(2,1)S(1)} %copy-done.1, bf16[128,4096]{1,0:T(8,128)(2,1)S(1)} %copy-done.2, ...), custom_call_target="tpu_custom_call" | custom-call | flops 1073741824 | bytes 2981888 | tf_op jit(solution)/shard_map/far_gradients/pallas_call | solution.py:175
  47.1 2.7 %collective-permute-start.4 = (bf16[256,512]{1,0:T(8,128)(2,1)S(1)}, bf16[256,512]{1,0:T(8,128)(2,1)S(1)}, u32[]{:S(2)}, u32[]{:S(2)}) collective-permute-start(bf16[256,512]{1,0:T(8,128)(2,1)S(1)} %get-tuple-element.24), channel_id=1, source_target_pairs={{2,0},{3,1},{4,2},{5,3},{6,4},{7,5},{8,6},{9,7},{10,8},{11,9},{12,... | collective-permute-start | bytes 786440 | tf_op jit(solution)/shard_map/ppermute | solution.py:23
  49.8 1.9 %collective-permute-start.6 = (bf16[256,512]{1,0:T(8,128)(2,1)S(1)}, bf16[256,512]{1,0:T(8,128)(2,1)S(1)}, u32[]{:S(2)}, u32[]{:S(2)}) collective-permute-start(bf16[256,512]{1,0:T(8,128)(2,1)S(1)} %get-tuple-element.26), channel_id=1, source_target_pairs={{2,0},{3,1},{4,2},{5,3},{6,4},{7,5},{8,6},{9,7},{10,8},{11,9},{12,... | collective-permute-start | bytes 786440 | tf_op jit(solution)/shard_map/ppermute | solution.py:23
  51.8 6.6 %near_gradients.1 = (bf16[128,4096]{1,0:T(8,128)(2,1)}, f32[256,512]{1,0:T(8,128)S(1)}, bf16[256,512]{1,0:T(8,128)(2,1)S(1)}, bf16[256,512]{1,0:T(8,128)(2,1)S(1)}) custom-call(bf16[128,4096]{1,0:T(8,128)(2,1)S(1)} %copy-done.1, bf16[128,4096]{1,0:T(8,128)(2,1)S(1)} %copy-done.2, bf16[272,512]{1,0:T(8,128)(2,1)S(1)} %pad_maximum_fusion.own_ref, ...), custom_call_target="tpu_custom_call" | custom-call | flops 2013265920 | bytes 5636096 | tf_op jit(solution)/shard_map/near_gradients/pallas_call | solution.py:175
  58.4 0.0 collective-permute-done.4
  58.4 0.1 add_convert_fusion.2
  58.5 5.6 %collective-permute-start.5 = (bf16[256,512]{1,0:T(8,128)(2,1)S(1)}, bf16[256,512]{1,0:T(8,128)(2,1)S(1)}, u32[]{:S(2)}, u32[]{:S(2)}) collective-permute-start(bf16[256,512]{1,0:T(8,128)(2,1)S(1)} %add_convert_fusion.2), channel_id=1, source_target_pairs={{2,0},{3,1},{4,2},{5,3},{6,4},{7,5},{8,6},{9,7},{10,8},{11,9},{12,... | collective-permute-start | bytes 786440 | tf_op jit(solution)/shard_map/ppermute | solution.py:23
  64.0 0.0 collective-permute-done.6
  64.1 0.1 add_convert_fusion.1
  64.1 3.5 %collective-permute-start.7 = (bf16[256,512]{1,0:T(8,128)(2,1)S(1)}, bf16[256,512]{1,0:T(8,128)(2,1)S(1)}, u32[]{:S(2)}, u32[]{:S(2)}) collective-permute-start(bf16[256,512]{1,0:T(8,128)(2,1)S(1)} %add_convert_fusion.1), channel_id=1, source_target_pairs={{1,0},{2,1},{3,2},{4,3},{5,4},{6,5},{7,6},{8,7},{9,8},{10,9},{11,1... | collective-permute-start | bytes 786440 | tf_op jit(solution)/shard_map/ppermute | solution.py:23
  67.7 3.1 %collective-permute-done.5 = bf16[256,512]{1,0:T(8,128)(2,1)S(1)} collective-permute-done((bf16[256,512]{1,0:T(8,128)(2,1)S(1)}, bf16[256,512]{1,0:T(8,128)(2,1)S(1)}, u32[]{:S(2)}, u32[]{:S(2)}) %collective-permute-start.5) | collective-permute-done | bytes 262176 | tf_op jit(solution)/shard_map/ppermute | solution.py:23
  70.7 2.8 %collective-permute-done.7 = bf16[256,512]{1,0:T(8,128)(2,1)S(1)} collective-permute-done((bf16[256,512]{1,0:T(8,128)(2,1)S(1)}, bf16[256,512]{1,0:T(8,128)(2,1)S(1)}, u32[]{:S(2)}, u32[]{:S(2)}) %collective-permute-start.7) | collective-permute-done | bytes 262176 | tf_op jit(solution)/shard_map/ppermute | solution.py:23
  73.5 0.1 add_convert_fusion
  73.6 0.7 fusion
  (2 shorter events, 0.0 us)
Async XLA Ops:
  2.3 20.1 %collective-permute-start.1 = (bf16[272,512]{1,0:T(8,128)(2,1)S(1)}, bf16[272,512]{1,0:T(8,128)(2,1)S(1)}, u32[]{:S(2)}, u32[]{:S(2)}) collective-permute-start(bf16[272,512]{1,0:T(8,128)(2,1)S(1)} %pad_maximum_fusion.own_ref), channel_id=1, source_target_pairs={{0,2},{1,3},{2,4},{3,5},{4,6},{5,7},{6,8},{7,9},{8,10},{9,11},{10,... | collective-permute-start | bytes 835592 | tf_op jit(solution)/shard_map/ppermute | solution.py:23
  6.1 22.1 %collective-permute-start = (bf16[272,512]{1,0:T(8,128)(2,1)S(1)}, bf16[272,512]{1,0:T(8,128)(2,1)S(1)}, u32[]{:S(2)}, u32[]{:S(2)}) collective-permute-start(bf16[272,512]{1,0:T(8,128)(2,1)S(1)} %pad_maximum_fusion.own_ref), channel_id=1, source_target_pairs={{0,1},{1,2},{2,3},{3,4},{4,5},{5,6},{6,7},{7,8},{8,9},{9,10},{10,1... | collective-permute-start | bytes 835592 | tf_op jit(solution)/shard_map/ppermute | solution.py:23
  22.4 14.3 %collective-permute-start.3 = (bf16[272,512]{1,0:T(8,128)(2,1)S(1)}, bf16[272,512]{1,0:T(8,128)(2,1)S(1)}, u32[]{:S(2)}, u32[]{:S(2)}) collective-permute-start(bf16[272,512]{1,0:T(8,128)(2,1)S(1)} %collective-permute-done.1.r2_ref), channel_id=1, source_target_pairs={{0,2},{1,3},{2,4},{3,5},{4,6},{5,7},{6,8},{7,9},{8,10},{9,11},{10,... | collective-permute-start | bytes 835592 | tf_op jit(solution)/shard_map/ppermute | solution.py:23
  28.2 14.0 %collective-permute-start.2 = (bf16[272,512]{1,0:T(8,128)(2,1)S(1)}, bf16[272,512]{1,0:T(8,128)(2,1)S(1)}, u32[]{:S(2)}, u32[]{:S(2)}) collective-permute-start(bf16[272,512]{1,0:T(8,128)(2,1)S(1)} %collective-permute-done.r1_ref), channel_id=1, source_target_pairs={{0,2},{1,3},{2,4},{3,5},{4,6},{5,7},{6,8},{7,9},{8,10},{9,11},{10,... | collective-permute-start | bytes 835592 | tf_op jit(solution)/shard_map/ppermute | solution.py:23
  30.1 1.2 %copy-start = (bf16[128,4096]{1,0:T(8,128)(2,1)S(1)}, bf16[128,4096]{1,0:T(8,128)(2,1)}, u32[]{:S(2)}) copy-start(bf16[128,4096]{1,0:T(8,128)(2,1)} %o_ref.1) | copy-start | bytes 3145732
  31.3 1.2 %copy-start.1 = (bf16[128,4096]{1,0:T(8,128)(2,1)S(1)}, bf16[128,4096]{1,0:T(8,128)(2,1)}, u32[]{:S(2)}) copy-start(bf16[128,4096]{1,0:T(8,128)(2,1)} %q_ref.5) | copy-start | bytes 3145732
  32.6 1.2 %copy-start.2 = (bf16[128,4096]{1,0:T(8,128)(2,1)S(1)}, bf16[128,4096]{1,0:T(8,128)(2,1)}, u32[]{:S(2)}) copy-start(bf16[128,4096]{1,0:T(8,128)(2,1)} %g_ref.5) | copy-start | bytes 3145732
  47.1 11.3 %collective-permute-start.4 = (bf16[256,512]{1,0:T(8,128)(2,1)S(1)}, bf16[256,512]{1,0:T(8,128)(2,1)S(1)}, u32[]{:S(2)}, u32[]{:S(2)}) collective-permute-start(bf16[256,512]{1,0:T(8,128)(2,1)S(1)} %get-tuple-element.24), channel_id=1, source_target_pairs={{2,0},{3,1},{4,2},{5,3},{6,4},{7,5},{8,6},{9,7},{10,8},{11,9},{12,... | collective-permute-start | bytes 786440 | tf_op jit(solution)/shard_map/ppermute | solution.py:23
  49.8 14.2 %collective-permute-start.6 = (bf16[256,512]{1,0:T(8,128)(2,1)S(1)}, bf16[256,512]{1,0:T(8,128)(2,1)S(1)}, u32[]{:S(2)}, u32[]{:S(2)}) collective-permute-start(bf16[256,512]{1,0:T(8,128)(2,1)S(1)} %get-tuple-element.26), channel_id=1, source_target_pairs={{2,0},{3,1},{4,2},{5,3},{6,4},{7,5},{8,6},{9,7},{10,8},{11,9},{12,... | collective-permute-start | bytes 786440 | tf_op jit(solution)/shard_map/ppermute | solution.py:23
  58.5 12.3 %collective-permute-start.5 = (bf16[256,512]{1,0:T(8,128)(2,1)S(1)}, bf16[256,512]{1,0:T(8,128)(2,1)S(1)}, u32[]{:S(2)}, u32[]{:S(2)}) collective-permute-start(bf16[256,512]{1,0:T(8,128)(2,1)S(1)} %add_convert_fusion.2), channel_id=1, source_target_pairs={{2,0},{3,1},{4,2},{5,3},{6,4},{7,5},{8,6},{9,7},{10,8},{11,9},{12,... | collective-permute-start | bytes 786440 | tf_op jit(solution)/shard_map/ppermute | solution.py:23
  64.1 9.4 %collective-permute-start.7 = (bf16[256,512]{1,0:T(8,128)(2,1)S(1)}, bf16[256,512]{1,0:T(8,128)(2,1)S(1)}, u32[]{:S(2)}, u32[]{:S(2)}) collective-permute-start(bf16[256,512]{1,0:T(8,128)(2,1)S(1)} %add_convert_fusion.1), channel_id=1, source_target_pairs={{1,0},{2,1},{3,2},{4,3},{5,4},{6,5},{7,6},{8,7},{9,8},{10,9},{11,1... | collective-permute-start | bytes 786440 | tf_op jit(solution)/shard_map/ppermute | solution.py:23

commit v3 on v2

v3 whole, which is shorter than its diff:
```python
import functools
import math

import jax
import jax.numpy as jnp
from jax import lax
from jax.experimental import pallas as pl
from jax.experimental.pallas import tpu as pltpu
from jax.sharding import PartitionSpec as P

HEAD_DIM = 128
MOST = 512
CHUNKS = 2
FULL1 = False
FULL2 = False
EARLY = True
LOG2_SCALE = HEAD_DIM ** (-0.5) * math.log2(math.e)
SCALE = HEAD_DIM ** (-0.5)
HIDDEN = -1e30
AXES = ("ctx", "head")
NT = (((1,), (1,)), ((), ()))
NN = (((1,), (0,)), ((), ()))


def shift(value, steps):
    count = lax.axis_size(AXES)
    return lax.ppermute(value, AXES, [(i, i + steps) for i in range(count) if 0 <= i + steps < count])


def dot(a, b, dims):
    return lax.dot_general(a, b, dims, preferred_element_type=jnp.float32)


def head_cols(h):
    return pl.ds(pl.multiple_of(h * HEAD_DIM, HEAD_DIM), HEAD_DIM)


def fill_bias(bias_scr, own, pieces, tok):
    def documents(piece):
        ref, base = piece
        rows = ref[base + 2 * tok : base + 2 * tok + 16, :tok].astype(jnp.float32)
        return jnp.concatenate([rows] * (tok // 16), axis=0)

    mine = documents(own)
    for at, piece in enumerate(pieces):
        same = documents(piece).T == mine
        if piece is own:
            key_at = lax.broadcasted_iota(jnp.int32, (tok, tok), 0)
            row_at = lax.broadcasted_iota(jnp.int32, (tok, tok), 1)
            same = same & (key_at <= row_at)
        bias_scr[at * tok : (at + 1) * tok, :] = jnp.where(same, 0.0, HIDDEN)


def stack(pieces, start, tok, cols):
    return jnp.concatenate([ref[base + start : base + start + tok, cols] for ref, base in pieces], axis=0)


def pair_rows(ref, first):
    return jnp.concatenate([ref[:, head_cols(first + i)] for i in range(2)], axis=0)


def pair_stat(ref, first):
    return jnp.concatenate([ref[pl.ds(first + i, 1), :] for i in range(2)], axis=1)


def put_stat(ref, first, value):
    tok = ref.shape[1]
    for i in range(2):
        ref[pl.ds(first + i, 1), :] = value[:, i * tok : (i + 1) * tok]


def near_stats_kernel(tok, group, kv_heads, offset, q_ref, g_ref, o_ref, own_ref, r1_ref, r2_ref, top_ref, sum_ref, delta_ref, bias_scr):
    own = (own_ref, 0)
    pieces = ((r2_ref, 0), (r1_ref, 0), own)
    fill_bias(bias_scr, own, pieces, tok)

    def one_kv_head(j, carry):
        keys = stack(pieces, 0, tok, head_cols(j))
        for pair in range(group // 2):
            first = j * group + 2 * pair
            bias = bias_scr[...]
            s = dot(keys, pair_rows(q_ref, offset + first), NT) + jnp.concatenate([bias, bias], axis=1)
            top = jnp.max(s, axis=0, keepdims=True)
            put_stat(top_ref, first, top)
            put_stat(sum_ref, first, jnp.sum(jnp.exp2((s - top) * LOG2_SCALE), axis=0, keepdims=True))
            prod = pair_rows(g_ref, offset + first).astype(jnp.float32) * pair_rows(o_ref, offset + first).astype(jnp.float32)
            put_stat(delta_ref, first, jnp.sum(prod.T, axis=0, keepdims=True))
        return carry

    lax.fori_loop(0, kv_heads, one_kv_head, 0, unroll=True)


def gradients(ds, p, q_ref, g_ref, first, group):
    q_all = jnp.concatenate([q_ref[:, head_cols(first + h)] for h in range(group)], axis=0)
    g_all = jnp.concatenate([g_ref[:, head_cols(first + h)] for h in range(group)], axis=0)
    return dot(ds, q_all, NN) * SCALE, dot(p, g_all, NN)


def put_gradients(outs, dk, dv, j, tok):
    for at, (out, base) in enumerate(outs):
        out[base : base + tok, head_cols(j)] = dk[at * tok : (at + 1) * tok].astype(out.dtype)
        out[base + tok : base + 2 * tok, head_cols(j)] = dv[at * tok : (at + 1) * tok].astype(out.dtype)


def far_kernel(
    tok, group, kv_heads, offset,
    q_ref, g_ref, own_ref, far_ref, near_top_ref, near_sum_ref, delta_ref,
    d43_ref, lse_ref, ds_ref,
    bias_scr, p_scr,
):
    pieces = ((far_ref, 0), (far_ref, far_ref.shape[0] // 2))
    fill_bias(bias_scr, (own_ref, 0), pieces, tok)

    def one_kv_head(j, carry):
        keys = stack(pieces, 0, tok, head_cols(j))
        values = stack(pieces, tok, tok, head_cols(j))
        for pair in range(group // 2):
            first = j * group + 2 * pair
            bias = bias_scr[...]
            s = dot(keys, pair_rows(q_ref, offset + first), NT) + jnp.concatenate([bias, bias], axis=1)
            near_top = pair_stat(near_top_ref, first)
            top = jnp.maximum(near_top, jnp.max(s, axis=0, keepdims=True))
            e = jnp.exp2((s - top) * LOG2_SCALE)
            total = pair_stat(near_sum_ref, first) * jnp.exp2((near_top - top) * LOG2_SCALE) + jnp.sum(e, axis=0, keepdims=True)
            inv = 1.0 / total
            put_stat(lse_ref, first, top * LOG2_SCALE + jnp.log2(total))
            prob = e * inv
            dprob = dot(values, pair_rows(g_ref, offset + first), NT)
            p_scr[:, 2 * pair * tok : 2 * (pair + 1) * tok] = prob.astype(jnp.bfloat16)
            low = (prob * (dprob - pair_stat(delta_ref, first))).astype(jnp.bfloat16)
            for i in range(2):
                ds_ref[:, head_cols(first + i)] = low[:, i * tok : (i + 1) * tok]
        cols = pl.ds(pl.multiple_of(j * group * HEAD_DIM, HEAD_DIM), group * HEAD_DIM)
        dk, dv = gradients(ds_ref[:, cols], p_scr[...], q_ref, g_ref, offset + j * group, group)
        put_gradients(((d43_ref, 0), (d43_ref, 2 * tok)), dk, dv, j, tok)
        return carry

    lax.fori_loop(0, kv_heads, one_kv_head, 0, unroll=True)


def middle_kernel(
    tok, group, kv_heads, offset,
    q_ref, g_ref, own_ref, r1_ref, r2_ref, lse_ref, delta_ref,
    d2_ref, d1_ref, ds_ref,
    bias_scr, p_scr,
):
    pieces = ((r2_ref, 0), (r1_ref, 0))
    fill_bias(bias_scr, (own_ref, 0), pieces, tok)

    def one_kv_head(j, carry):
        scores_gradient(pieces, bias_scr, p_scr, ds_ref, q_ref, g_ref, lse_ref, delta_ref, j, tok, group, offset)
        cols = pl.ds(pl.multiple_of(j * group * HEAD_DIM, HEAD_DIM), group * HEAD_DIM)
        dk, dv = gradients(ds_ref[:, cols], p_scr[...], q_ref, g_ref, offset + j * group, group)
        put_gradients(((d2_ref, 0), (d1_ref, 0)), dk, dv, j, tok)
        return carry

    lax.fori_loop(0, kv_heads, one_kv_head, 0, unroll=True)


def scores_gradient(pieces, bias_scr, p_scr, ds_ref, q_ref, g_ref, lse_ref, delta_ref, j, tok, group, offset):
    keys = stack(pieces, 0, tok, head_cols(j))
    values = stack(pieces, tok, tok, head_cols(j))
    for pair in range(group // 2):
        first = j * group + 2 * pair
        bias = bias_scr[...]
        s = dot(keys, pair_rows(q_ref, offset + first), NT) + jnp.concatenate([bias, bias], axis=1)
        prob = jnp.exp2(s * LOG2_SCALE - pair_stat(lse_ref, first))
        dprob = dot(values, pair_rows(g_ref, offset + first), NT)
        p_scr[:, 2 * pair * tok : 2 * (pair + 1) * tok] = prob.astype(jnp.bfloat16)
        low = (prob * (dprob - pair_stat(delta_ref, first))).astype(jnp.bfloat16)
        for i in range(2):
            ds_ref[:, head_cols(first + i)] = low[:, i * tok : (i + 1) * tok]


def own_kernel(
    tok, group, kv_heads, offset,
    q_ref, g_ref, own_ref, r1_ref, r2_ref, far_ref, lse_ref, delta_ref, far_ds_ref, middle_ds_ref,
    dq_ref, own_out,
    bias_scr, p_scr, ds_scr,
):
    own = (own_ref, 0)
    fill_bias(bias_scr, own, (own,), tok)

    def one_kv_head(j, carry):
        scores_gradient((own,), bias_scr, p_scr, ds_scr, q_ref, g_ref, lse_ref, delta_ref, j, tok, group, offset)
        cols = pl.ds(pl.multiple_of(j * group * HEAD_DIM, HEAD_DIM), group * HEAD_DIM)
        dk, dv = gradients(ds_scr[:, cols], p_scr[...], q_ref, g_ref, offset + j * group, group)
        put_gradients(((own_out, 0),), dk, dv, j, tok)
        every = ((far_ref, 0), (far_ref, far_ref.shape[0] // 2), (r2_ref, 0), (r1_ref, 0), own)
        keys_t = jnp.concatenate([ref[base : base + tok, head_cols(j)].T for ref, base in every], axis=1)
        ds_all = jnp.concatenate([far_ds_ref[:, cols], middle_ds_ref[:, cols], ds_scr[:, cols]], axis=0)
        dq_t = dot(keys_t, ds_all, NN) * SCALE
        for h in range(group):
            dq_ref[:, head_cols(j * group + h)] = dq_t[:, h * tok : (h + 1) * tok].T.astype(jnp.bfloat16)
        return carry

    lax.fori_loop(0, kv_heads, one_kv_head, 0, unroll=True)


def call(kernel, name, args, out_shape, scratch, keys, products, sizes):
    tok, group, kv_heads, _ = sizes
    whole = pl.BlockSpec(memory_space=pltpu.VMEM)
    pairs = keys * tok * group * kv_heads
    return pl.pallas_call(
        functools.partial(kernel, *sizes),
        in_specs=[whole] * len(args),
        out_specs=tuple(whole for _ in out_shape),
        out_shape=tuple(jax.ShapeDtypeStruct(s, d) for s, d in out_shape),
        scratch_shapes=[pltpu.VMEM(s, d) for s, d in scratch],
        compiler_params=pltpu.CompilerParams(vmem_limit_bytes=40 * 2**20),
        cost_estimate=pl.CostEstimate(
            flops=2 * products * pairs * HEAD_DIM, bytes_accessed=sum(a.size * a.dtype.itemsize for a in args), transcendentals=pairs
        ),
        name=name,
    )(*args)


def per_device(query, key, value, attn_out, out_grad, segments):
    tok = query.shape[0]
    heads = query.shape[1] // HEAD_DIM // CHUNKS
    width = key.shape[1] // CHUNKS
    kv_heads = width // HEAD_DIM
    group = heads // kv_heads
    f32, bf16 = jnp.float32, jnp.bfloat16
    documents = jnp.tile((segments + 1).astype(bf16)[None, :], (16, width // tok))
    stat = ((heads, tok), f32)
    near, far = 3 * tok, 2 * tok
    parts = range(CHUNKS)
    sizes = [(tok, group, kv_heads, c * heads) for c in parts]
    cols = [slice(c * width, (c + 1) * width) for c in parts]
    if FULL1:
        whole_own = jnp.concatenate([key, value, jnp.tile(documents, (1, CHUNKS))], axis=0)
        whole_r2 = shift(whole_own, 2)
        whole_r1 = shift(whole_own, 1)
        own, r2, r1 = ([a[:, cols[c]] for c in parts] for a in (whole_own, whole_r2, whole_r1))
    else:
        own = [jnp.concatenate([key[:, cols[c]], value[:, cols[c]], documents], axis=0) for c in parts]
        r2 = [shift(own[c], 2) for c in parts]
        r1 = [shift(own[c], 1) for c in parts]
    near_out, r43 = [], []
    for c in parts:
        relayed = jnp.concatenate([r2[c], r1[c]], axis=0)
        if near_out and EARLY:
            relayed, _ = lax.optimization_barrier((relayed, near_out[-1]))
        r43.append(shift(relayed, 2))
        near_out.append(call(
            near_stats_kernel, "near_stats", (query, out_grad, attn_out, own[c], r1[c], r2[c]),
            (stat, stat, stat), (((near, tok), f32),), near, 1, sizes[c],
        ))
    pending = ((2 * tok, width), bf16)
    saved = ((far, heads * tok), bf16)
    far_out, x43 = [], []
    for c in parts:
        near_top, near_sum, delta = near_out[c]
        far_out.append(call(
            far_kernel, "far_gradients", (query, out_grad, own[c], r43[c], near_top, near_sum, delta),
            (((4 * tok, width), bf16), stat, saved),
            (((far, tok), f32), ((far, group * tok), bf16)), far, 4, sizes[c],
        ))
        x43.append(shift(far_out[c][0], -2))
    sums, middle_ds = [], []
    for c in parts:
        lse = far_out[c][1]
        if sums and not FULL2:
            lse, _ = lax.optimization_barrier((lse, sums[-1]))
        d2, d1, ds = call(
            middle_kernel, "near_middle", (query, out_grad, own[c], r1[c], r2[c], lse, near_out[c][2]),
            (pending, pending, saved), (((far, tok), f32), ((far, group * tok), bf16)), far, 4, sizes[c],
        )
        middle_ds.append(ds)
        sums.append((
            (d2.astype(f32) + x43[c][: 2 * tok].astype(f32)).astype(bf16),
            (d1.astype(f32) + x43[c][2 * tok :].astype(f32)).astype(bf16),
        ))
    if FULL2:
        sums = [tuple(jnp.concatenate(a, axis=1) for a in zip(*sums))]
        sums = lax.optimization_barrier(sums)
    back = [(shift(sum2, -2), shift(sum1, -1)) for sum2, sum1 in sums]
    dq, mine = [], []
    for c in parts:
        lse, _ = lax.optimization_barrier((far_out[c][1], sums[-1]))
        query_grad, terms = call(
            own_kernel, "near_own",
            (query, out_grad, own[c], r1[c], r2[c], r43[c], lse, near_out[c][2], far_out[c][2], middle_ds[c]),
            (((tok, heads * HEAD_DIM), bf16), ((2 * tok, width), f32)),
            (((tok, tok), f32), ((tok, group * tok), bf16), ((tok, heads * tok), bf16)), tok, 9, sizes[c],
        )
        dq.append(query_grad)
        mine.append(terms)
    if FULL2:
        mine = [jnp.concatenate(mine, axis=1)]
    total = [(m + y2.astype(f32) + y1.astype(f32)).astype(bf16) for m, (y2, y1) in zip(mine, back)]
    total = lax.optimization_barrier(jnp.concatenate(total, axis=1))
    return jnp.concatenate(dq, axis=1), total[:tok], total[tok:]


def solution(mesh):
    split = P(AXES, None)
    return jax.shard_map(
        per_device,
        mesh=mesh,
        in_specs=(split, split, split, split, split, P(AXES)),
        out_specs=(split, split, split),
        check_vma=False,
    )
```

time: 74.8 us -> 69 us (0.922)
  waiting for transfers between devices: 28 us -> 13.2 us
  starting transfers between devices: 24.9 us -> 35.8 us
  Pallas kernels: 14.5 us -> 12.3 us
    ppermute x8 -> x12, waiting for transfers between devices: 28 us -> 13.2 us  [shift(): lax.ppermute(value, AXES, [(i, i + steps) for i in range(count) if 0 <= i...]
    ppermute x8 -> x12, starting transfers between devices: 24.9 us -> 35.8 us  [shift(): lax.ppermute(value, AXES, [(i, i + steps) for i in range(count) if 0 <= i...]
    pallas_call x3 -> x8, Pallas kernels: 14.5 us -> 12.3 us  [call(): pl.pallas_call(functools.partial(kernel, *sizes), in_specs=[whole] * len(...]
    unnamed x6, local copies, waits for them, and re-layouts: 3.67 us -> 2.45 us
    slice x1 -> x2, local copies, waits for them, and re-layouts: 0.72 us -> 1.67 us  [the longest x1 0.95 us: per_device(): key[:, cols[c]]]
  transfers between devices with their start and end apart: 8 -> 12, of which waited for: 5 -> 6; matrix products, arithmetic and copies ran while one was open for 0% -> 2% of each run, Pallas kernels for 13% -> 18%
where the time goes in v3:
time: 69 us; the launch traced here: 68.4 us
  starting transfers between devices  35.8 us (52%)
  waiting for transfers between devices  13.2 us (19%)
  Pallas kernels  12.3 us (18%)
  local copies, waits for them, and re-layouts  4.13 us (6%)
  other arithmetic  2.11 us (3%)
  between operations  0.87 us (1%)
    ppermute x12, starting transfers between devices, shift(): lax.ppermute(value, AXES, [(i, i + steps) for i in range(count) if 0 <= i...  35.8 us
    ppermute x12, waiting for transfers between devices, shift(): lax.ppermute(value, AXES, [(i, i + steps) for i in range(count) if 0 <= i...  13.2 us
    pallas_call x8, Pallas kernels, call(): pl.pallas_call(functools.partial(kernel, *sizes), in_specs=[whole] * len(...  12.3 us
    unnamed x6, local copies, waits for them, and re-layouts  2.45 us
  transfers between devices with their start and end apart: 12, of which 6 were waited for; matrix products, arithmetic and copies ran while one was open for 2% of the time, Pallas kernels for 18%

profile of v3, /device:TPU:6, one launch (start us, length us, event | category | flops | bytes accessed | tf_op | source)
XLA Modules:
  0.0 68.4 jit_solution(16489484976118981533)
XLA Ops:
  0.6 0.0 copy-start
  0.6 0.7 %add_convert_fusion.6 = bf16[128]{0:T(256)(128)(2,1)S(1)} fusion(s32[128]{0:T(128)} %param.11), kind=kLoop, calls=%fused_computation.12 | loop fusion | flops 256 | bytes 768 | tf_op jit(solution)/shard_map/convert_element_type | solution.py:225
  1.4 1.0 %fusion.1 = (bf16[128,256]{1,0:T(8,128)(2,1)S(1)}, bf16[128,256]{1,0:T(8,128)(2,1)S(1)}, bf16[128,256]{1,0:T(8,128)(2,1)S(1)}, bf16[128,256]{1,0:T(8,128)(2,1)S(1)}) fusion(bf16[128,512]{1,0:T(8,128)(2,1)} %param.7, bf16[128,512]{1,0:T(8,128)(2,1)} %param.8), kind=kLoop, calls=%fused_computation.15 | loop fusion | bytes 524288 | tf_op jit(solution)/shard_map/slice | solution.py:237
  2.4 3.8 %collective-permute-start.1 = (bf16[272,256]{1,0:T(8,128)(2,1)S(1)}, bf16[272,256]{1,0:T(8,128)(2,1)S(1)}, u32[]{:S(2)}, u32[]{:S(2)}) collective-permute-start(bf16[272,256]{1,0:T(8,128)(2,1)S(1)} %get-tuple-element.65.own_ref), channel_id=1, source_target_pairs={{0,2},{1,3},{2,4},{3,5},{4,6},{5,7},{6,8},{7,9},{8,10},{9,11},{10,... | collective-permute-start | bytes 417800 | tf_op jit(solution)/shard_map/ppermute | solution.py:27
  6.2 3.5 %collective-permute-start = (bf16[272,256]{1,0:T(8,128)(2,1)S(1)}, bf16[272,256]{1,0:T(8,128)(2,1)S(1)}, u32[]{:S(2)}, u32[]{:S(2)}) collective-permute-start(bf16[272,256]{1,0:T(8,128)(2,1)S(1)} %get-tuple-element.65.own_ref), channel_id=1, source_target_pairs={{0,1},{1,2},{2,3},{3,4},{4,5},{5,6},{6,7},{7,8},{8,9},{9,10},{10,1... | collective-permute-start | bytes 417800 | tf_op jit(solution)/shard_map/ppermute | solution.py:27
  9.7 3.8 %collective-permute-start.4 = (bf16[272,256]{1,0:T(8,128)(2,1)S(1)}, bf16[272,256]{1,0:T(8,128)(2,1)S(1)}, u32[]{:S(2)}, u32[]{:S(2)}) collective-permute-start(bf16[272,256]{1,0:T(8,128)(2,1)S(1)} %get-tuple-element.66.own_ref), channel_id=1, source_target_pairs={{0,2},{1,3},{2,4},{3,5},{4,6},{5,7},{6,8},{7,9},{8,10},{9,11},{10,... | collective-permute-start | bytes 417800 | tf_op jit(solution)/shard_map/ppermute | solution.py:27
  13.6 3.7 %collective-permute-start.3 = (bf16[272,256]{1,0:T(8,128)(2,1)S(1)}, bf16[272,256]{1,0:T(8,128)(2,1)S(1)}, u32[]{:S(2)}, u32[]{:S(2)}) collective-permute-start(bf16[272,256]{1,0:T(8,128)(2,1)S(1)} %get-tuple-element.66.own_ref), channel_id=1, source_target_pairs={{0,1},{1,2},{2,3},{3,4},{4,5},{5,6},{6,7},{7,8},{8,9},{9,10},{10,1... | collective-permute-start | bytes 417800 | tf_op jit(solution)/shard_map/ppermute | solution.py:27
  17.3 2.2 %collective-permute-done.1.r2_ref = bf16[272,256]{1,0:T(8,128)(2,1)S(1)} collective-permute-done((bf16[272,256]{1,0:T(8,128)(2,1)S(1)}, bf16[272,256]{1,0:T(8,128)(2,1)S(1)}, u32[]{:S(2)}, u32[]{:S(2)}) %collective-permute-start.1) | collective-permute-done | bytes 139296 | tf_op jit(solution)/shard_map/ppermute | solution.py:27
  19.5 2.8 %collective-permute-done.r1_ref = bf16[272,256]{1,0:T(8,128)(2,1)S(1)} collective-permute-done((bf16[272,256]{1,0:T(8,128)(2,1)S(1)}, bf16[272,256]{1,0:T(8,128)(2,1)S(1)}, u32[]{:S(2)}, u32[]{:S(2)}) %collective-permute-start) | collective-permute-done | bytes 139296 | tf_op jit(solution)/shard_map/ppermute | solution.py:27
  22.3 1.9 %collective-permute-start.2 = (bf16[544,256]{1,0:T(8,128)(2,1)S(1)}, bf16[544,256]{1,0:T(8,128)(2,1)S(1)}, u32[]{:S(2)}, u32[]{:S(2)}) collective-permute-start(bf16[544,256]{1,0:T(8,128)(2,1)S(1)} %pad_maximum_fusion.1), channel_id=1, source_target_pairs={{0,2},{1,3},{2,4},{3,5},{4,6},{5,7},{6,8},{7,9},{8,10},{9,11},{10,... | collective-permute-start | bytes 835592 | tf_op jit(solution)/shard_map/ppermute | solution.py:27
  24.3 0.0 copy-done
  24.3 0.0 copy-start.1
  24.3 1.2 %copy-done.1 = bf16[128,4096]{1,0:T(8,128)(2,1)S(1)} copy-done((bf16[128,4096]{1,0:T(8,128)(2,1)S(1)}, bf16[128,4096]{1,0:T(8,128)(2,1)}, u32[]{:S(2)}) %copy-start.1) | copy-done | bytes 1048600
  25.5 0.0 copy-start.2
  25.5 1.2 %copy-done.2 = bf16[128,4096]{1,0:T(8,128)(2,1)S(1)} copy-done((bf16[128,4096]{1,0:T(8,128)(2,1)S(1)}, bf16[128,4096]{1,0:T(8,128)(2,1)}, u32[]{:S(2)}) %copy-start.2) | copy-done | bytes 1048600
  26.7 1.2 %near_stats.2 = (f32[16,128]{1,0:T(8,128)S(1)}, f32[16,128]{1,0:T(8,128)S(1)}, f32[16,128]{1,0:T(8,128)S(1)}) custom-call(bf16[128,4096]{1,0:T(8,128)(2,1)S(1)} %copy-done, bf16[128,4096]{1,0:T(8,128)(2,1)S(1)} %copy-done.1, bf16[128,4096]{1,0:T(8,128)(2,1)S(1)} %copy-done.2, bf16[272,256]{1,0:T(8,128)(2,1)S(1)} %get-tuple-element.65.own_ref, ...), custom_call_target="tpu_custom_call" | custom-call | flops 201326592 | bytes 3563520 | tf_op jit(solution)/shard_map/near_stats/pallas_call | solution.py:204
  28.0 0.0 collective-permute-done.4.r2_ref
  28.0 0.3 collective-permute-done.3.r1_ref
  28.3 1.9 %collective-permute-start.5 = (bf16[544,256]{1,0:T(8,128)(2,1)S(1)}, bf16[544,256]{1,0:T(8,128)(2,1)S(1)}, u32[]{:S(2)}, u32[]{:S(2)}) collective-permute-start(bf16[544,256]{1,0:T(8,128)(2,1)S(1)} %pad_maximum_fusion.2), channel_id=1, source_target_pairs={{0,2},{1,3},{2,4},{3,5},{4,6},{5,7},{6,8},{7,9},{8,10},{9,11},{10,... | collective-permute-start | bytes 835592 | tf_op jit(solution)/shard_map/ppermute | solution.py:27
  30.2 6.9 %collective-permute-done.2.far_ref = bf16[544,256]{1,0:T(8,128)(2,1)S(1)} collective-permute-done((bf16[544,256]{1,0:T(8,128)(2,1)S(1)}, bf16[544,256]{1,0:T(8,128)(2,1)S(1)}, u32[]{:S(2)}, u32[]{:S(2)}) %collective-permute-start.2) | collective-permute-done | bytes 278560 | tf_op jit(solution)/shard_map/ppermute | solution.py:27
  37.2 2.1 %far_gradients.2 = (bf16[512,256]{1,0:T(8,128)(2,1)S(1)}, f32[16,128]{1,0:T(8,128)S(1)}, bf16[256,2048]{1,0:T(8,128)(2,1)S(1)}) custom-call(bf16[128,4096]{1,0:T(8,128)(2,1)S(1)} %copy-done, bf16[128,4096]{1,0:T(8,128)(2,1)S(1)} %copy-done.1, bf16[272,256]{1,0:T(8,128)(2,1)S(1)} %get-tuple-element.65.own_ref, ...), custom_call_target="tpu_custom_call" | custom-call | flops 536870912 | bytes 2539520 | tf_op jit(solution)/shard_map/far_gradients/pallas_call | solution.py:204
  39.3 1.9 %collective-permute-start.6 = (bf16[512,256]{1,0:T(8,128)(2,1)S(1)}, bf16[512,256]{1,0:T(8,128)(2,1)S(1)}, u32[]{:S(2)}, u32[]{:S(2)}) collective-permute-start(bf16[512,256]{1,0:T(8,128)(2,1)S(1)} %get-tuple-element.39), channel_id=1, source_target_pairs={{2,0},{3,1},{4,2},{5,3},{6,4},{7,5},{8,6},{9,7},{10,8},{11,9},{12,... | collective-permute-start | bytes 786440 | tf_op jit(solution)/shard_map/ppermute | solution.py:27
  41.2 1.2 %near_stats.3 = (f32[16,128]{1,0:T(8,128)S(1)}, f32[16,128]{1,0:T(8,128)S(1)}, f32[16,128]{1,0:T(8,128)S(1)}) custom-call(bf16[128,4096]{1,0:T(8,128)(2,1)S(1)} %copy-done, bf16[128,4096]{1,0:T(8,128)(2,1)S(1)} %copy-done.1, bf16[128,4096]{1,0:T(8,128)(2,1)S(1)} %copy-done.2, bf16[272,256]{1,0:T(8,128)(2,1)S(1)} %get-tuple-element.66.own_ref, ...), custom_call_target="tpu_custom_call" | custom-call | flops 201326592 | bytes 3563520 | tf_op jit(solution)/shard_map/near_stats/pallas_call | solution.py:204
  42.4 0.5 collective-permute-done.5.far_ref
  42.9 2.1 %far_gradients.3 = (bf16[512,256]{1,0:T(8,128)(2,1)S(1)}, f32[16,128]{1,0:T(8,128)S(1)}, bf16[256,2048]{1,0:T(8,128)(2,1)S(1)}) custom-call(bf16[128,4096]{1,0:T(8,128)(2,1)S(1)} %copy-done, bf16[128,4096]{1,0:T(8,128)(2,1)S(1)} %copy-done.1, bf16[272,256]{1,0:T(8,128)(2,1)S(1)} %get-tuple-element.66.own_ref, ...), custom_call_target="tpu_custom_call" | custom-call | flops 536870912 | bytes 2539520 | tf_op jit(solution)/shard_map/far_gradients/pallas_call | solution.py:204
  45.0 3.4 %collective-permute-start.7 = (bf16[512,256]{1,0:T(8,128)(2,1)S(1)}, bf16[512,256]{1,0:T(8,128)(2,1)S(1)}, u32[]{:S(2)}, u32[]{:S(2)}) collective-permute-start(bf16[512,256]{1,0:T(8,128)(2,1)S(1)} %get-tuple-element.43), channel_id=1, source_target_pairs={{2,0},{3,1},{4,2},{5,3},{6,4},{7,5},{8,6},{9,7},{10,8},{11,9},{12,... | collective-permute-start | bytes 786440 | tf_op jit(solution)/shard_map/ppermute | solution.py:27
  48.4 1.4 %near_middle.2 = (bf16[256,256]{1,0:T(8,128)(2,1)S(1)}, bf16[256,256]{1,0:T(8,128)(2,1)S(1)}, bf16[256,2048]{1,0:T(8,128)(2,1)S(1)}) custom-call(bf16[128,4096]{1,0:T(8,128)(2,1)S(1)} %copy-done, bf16[128,4096]{1,0:T(8,128)(2,1)S(1)} %copy-done.1, bf16[272,256]{1,0:T(8,128)(2,1)S(1)} %get-tuple-element.65.own_ref, ...), custom_call_target="tpu_custom_call" | custom-call | flops 536870912 | bytes 2531328 | tf_op jit(solution)/shard_map/near_middle/pallas_call | solution.py:204
  49.8 0.0 collective-permute-done.6
  49.8 0.1 add_convert_fusion.4
  49.8 4.6 %collective-permute-start.9 = (bf16[256,256]{1,0:T(8,128)(2,1)S(1)}, bf16[256,256]{1,0:T(8,128)(2,1)S(1)}, u32[]{:S(2)}, u32[]{:S(2)}) collective-permute-start(bf16[256,256]{1,0:T(8,128)(2,1)S(1)} %get-tuple-element.59), channel_id=1, source_target_pairs={{1,0},{2,1},{3,2},{4,3},{5,4},{6,5},{7,6},{8,7},{9,8},{10,9},{11,1... | collective-permute-start | bytes 393224 | tf_op jit(solution)/shard_map/ppermute | solution.py:27
  54.4 1.9 %collective-permute-start.8 = (bf16[256,256]{1,0:T(8,128)(2,1)S(1)}, bf16[256,256]{1,0:T(8,128)(2,1)S(1)}, u32[]{:S(2)}, u32[]{:S(2)}) collective-permute-start(bf16[256,256]{1,0:T(8,128)(2,1)S(1)} %get-tuple-element.60), channel_id=1, source_target_pairs={{2,0},{3,1},{4,2},{5,3},{6,4},{7,5},{8,6},{9,7},{10,8},{11,9},{12,... | collective-permute-start | bytes 393224 | tf_op jit(solution)/shard_map/ppermute | solution.py:27
  56.3 1.4 %near_middle.3 = (bf16[256,256]{1,0:T(8,128)(2,1)S(1)}, bf16[256,256]{1,0:T(8,128)(2,1)S(1)}, bf16[256,2048]{1,0:T(8,128)(2,1)S(1)}) custom-call(bf16[128,4096]{1,0:T(8,128)(2,1)S(1)} %copy-done, bf16[128,4096]{1,0:T(8,128)(2,1)S(1)} %copy-done.1, bf16[272,256]{1,0:T(8,128)(2,1)S(1)} %get-tuple-element.66.own_ref, ...), custom_call_target="tpu_custom_call" | custom-call | flops 536870912 | bytes 2531328 | tf_op jit(solution)/shard_map/near_middle/pallas_call | solution.py:204
  57.7 0.0 collective-permute-done.7
  57.7 0.1 add_convert_fusion.2
  57.8 2.9 %collective-permute-start.11 = (bf16[256,256]{1,0:T(8,128)(2,1)S(1)}, bf16[256,256]{1,0:T(8,128)(2,1)S(1)}, u32[]{:S(2)}, u32[]{:S(2)}) collective-permute-start(bf16[256,256]{1,0:T(8,128)(2,1)S(1)} %get-tuple-element.57), channel_id=1, source_target_pairs={{1,0},{2,1},{3,2},{4,3},{5,4},{6,5},{7,6},{8,7},{9,8},{10,9},{11,1... | collective-permute-start | bytes 393224 | tf_op jit(solution)/shard_map/ppermute | solution.py:27
  60.7 2.5 %collective-permute-start.10 = (bf16[256,256]{1,0:T(8,128)(2,1)S(1)}, bf16[256,256]{1,0:T(8,128)(2,1)S(1)}, u32[]{:S(2)}, u32[]{:S(2)}) collective-permute-start(bf16[256,256]{1,0:T(8,128)(2,1)S(1)} %get-tuple-element.58), channel_id=1, source_target_pairs={{2,0},{3,1},{4,2},{5,3},{6,4},{7,5},{8,6},{9,7},{10,8},{11,9},{12,... | collective-permute-start | bytes 393224 | tf_op jit(solution)/shard_map/ppermute | solution.py:27
  63.2 1.4 %near_own.3 = (bf16[128,2048]{1,0:T(8,128)(2,1)S(1)}, f32[256,256]{1,0:T(8,128)S(1)}) custom-call(bf16[128,4096]{1,0:T(8,128)(2,1)S(1)} %copy-done, bf16[128,4096]{1,0:T(8,128)(2,1)S(1)} %copy-done.1, bf16[272,256]{1,0:T(8,128)(2,1)S(1)} %get-tuple-element.66.own_ref, bf16[272,256]{1,0:T(8,128)(2,1)S(1)} %collective-permute-done.3.r1_ref, ...), custom_call_target="tpu_custom_call" | custom-call | flops 603979776 | bytes 4907008 | tf_op jit(solution)/shard_map/near_own/pallas_call | solution.py:204
  64.7 1.4 %near_own.2 = (bf16[128,2048]{1,0:T(8,128)(2,1)S(1)}, f32[256,256]{1,0:T(8,128)S(1)}) custom-call(bf16[128,4096]{1,0:T(8,128)(2,1)S(1)} %copy-done, bf16[128,4096]{1,0:T(8,128)(2,1)S(1)} %copy-done.1, bf16[272,256]{1,0:T(8,128)(2,1)S(1)} %get-tuple-element.65.own_ref, bf16[272,256]{1,0:T(8,128)(2,1)S(1)} %collective-permute-done.r1_ref, ...), custom_call_target="tpu_custom_call" | custom-call | flops 603979776 | bytes 4907008 | tf_op jit(solution)/shard_map/near_own/pallas_call | solution.py:204
  66.1 1.0 %pad_maximum_fusion = bf16[128,4096]{1,0:T(8,128)(2,1)} fusion(bf16[128,2048]{1,0:T(8,128)(2,1)S(1)} %get-tuple-element.52, bf16[128,2048]{1,0:T(8,128)(2,1)S(1)} %get-tuple-element.48), kind=kLoop, calls=%fused_computation | loop fusion | flops 2097152 | bytes 2097152 | tf_op jit(solution)/shard_map/concatenate | solution.py:294
  67.2 0.0 collective-permute-done.9
  67.2 0.0 collective-permute-done.8
  67.2 0.1 add_convert_fusion.1
  67.2 0.0 collective-permute-done.11
  67.2 0.4 collective-permute-done.10
  67.7 0.7 %fusion = (bf16[128,512]{1,0:T(8,128)(2,1)}, bf16[128,512]{1,0:T(8,128)(2,1)}) fusion(bf16[256,512]{1,0:T(8,128)(2,1)S(1)} %pad_maximum_fusion.3), kind=kLoop, calls=%fused_computation.14 | loop fusion | bytes 524288 | tf_op jit(solution)/shard_map/slice | solution.py:294
  (7 shorter events, 0.1 us)
Async XLA Ops:
  0.6 23.6 %copy-start = (bf16[128,4096]{1,0:T(8,128)(2,1)S(1)}, bf16[128,4096]{1,0:T(8,128)(2,1)}, u32[]{:S(2)}) copy-start(bf16[128,4096]{1,0:T(8,128)(2,1)} %q_ref.15) | copy-start | bytes 3145732
  2.4 17.1 %collective-permute-start.1 = (bf16[272,256]{1,0:T(8,128)(2,1)S(1)}, bf16[272,256]{1,0:T(8,128)(2,1)S(1)}, u32[]{:S(2)}, u32[]{:S(2)}) collective-permute-start(bf16[272,256]{1,0:T(8,128)(2,1)S(1)} %get-tuple-element.65.own_ref), channel_id=1, source_target_pairs={{0,2},{1,3},{2,4},{3,5},{4,6},{5,7},{6,8},{7,9},{8,10},{9,11},{10,... | collective-permute-start | bytes 417800 | tf_op jit(solution)/shard_map/ppermute | solution.py:27
  6.2 16.1 %collective-permute-start = (bf16[272,256]{1,0:T(8,128)(2,1)S(1)}, bf16[272,256]{1,0:T(8,128)(2,1)S(1)}, u32[]{:S(2)}, u32[]{:S(2)}) collective-permute-start(bf16[272,256]{1,0:T(8,128)(2,1)S(1)} %get-tuple-element.65.own_ref), channel_id=1, source_target_pairs={{0,1},{1,2},{2,3},{3,4},{4,5},{5,6},{6,7},{7,8},{8,9},{9,10},{10,1... | collective-permute-start | bytes 417800 | tf_op jit(solution)/shard_map/ppermute | solution.py:27
  9.7 18.3 %collective-permute-start.4 = (bf16[272,256]{1,0:T(8,128)(2,1)S(1)}, bf16[272,256]{1,0:T(8,128)(2,1)S(1)}, u32[]{:S(2)}, u32[]{:S(2)}) collective-permute-start(bf16[272,256]{1,0:T(8,128)(2,1)S(1)} %get-tuple-element.66.own_ref), channel_id=1, source_target_pairs={{0,2},{1,3},{2,4},{3,5},{4,6},{5,7},{6,8},{7,9},{8,10},{9,11},{10,... | collective-permute-start | bytes 417800 | tf_op jit(solution)/shard_map/ppermute | solution.py:27
  13.6 14.7 %collective-permute-start.3 = (bf16[272,256]{1,0:T(8,128)(2,1)S(1)}, bf16[272,256]{1,0:T(8,128)(2,1)S(1)}, u32[]{:S(2)}, u32[]{:S(2)}) collective-permute-start(bf16[272,256]{1,0:T(8,128)(2,1)S(1)} %get-tuple-element.66.own_ref), channel_id=1, source_target_pairs={{0,1},{1,2},{2,3},{3,4},{4,5},{5,6},{6,7},{7,8},{8,9},{9,10},{10,1... | collective-permute-start | bytes 417800 | tf_op jit(solution)/shard_map/ppermute | solution.py:27
  22.3 14.8 %collective-permute-start.2 = (bf16[544,256]{1,0:T(8,128)(2,1)S(1)}, bf16[544,256]{1,0:T(8,128)(2,1)S(1)}, u32[]{:S(2)}, u32[]{:S(2)}) collective-permute-start(bf16[544,256]{1,0:T(8,128)(2,1)S(1)} %pad_maximum_fusion.1), channel_id=1, source_target_pairs={{0,2},{1,3},{2,4},{3,5},{4,6},{5,7},{6,8},{7,9},{8,10},{9,11},{10,... | collective-permute-start | bytes 835592 | tf_op jit(solution)/shard_map/ppermute | solution.py:27
  24.3 1.2 %copy-start.1 = (bf16[128,4096]{1,0:T(8,128)(2,1)S(1)}, bf16[128,4096]{1,0:T(8,128)(2,1)}, u32[]{:S(2)}) copy-start(bf16[128,4096]{1,0:T(8,128)(2,1)} %g_ref.15) | copy-start | bytes 3145732
  25.5 1.2 %copy-start.2 = (bf16[128,4096]{1,0:T(8,128)(2,1)S(1)}, bf16[128,4096]{1,0:T(8,128)(2,1)}, u32[]{:S(2)}) copy-start(bf16[128,4096]{1,0:T(8,128)(2,1)} %o_ref.3) | copy-start | bytes 3145732
  28.3 14.6 %collective-permute-start.5 = (bf16[544,256]{1,0:T(8,128)(2,1)S(1)}, bf16[544,256]{1,0:T(8,128)(2,1)S(1)}, u32[]{:S(2)}, u32[]{:S(2)}) collective-permute-start(bf16[544,256]{1,0:T(8,128)(2,1)S(1)} %pad_maximum_fusion.2), channel_id=1, source_target_pairs={{0,2},{1,3},{2,4},{3,5},{4,6},{5,7},{6,8},{7,9},{8,10},{9,11},{10,... | collective-permute-start | bytes 835592 | tf_op jit(solution)/shard_map/ppermute | solution.py:27
  39.3 10.5 %collective-permute-start.6 = (bf16[512,256]{1,0:T(8,128)(2,1)S(1)}, bf16[512,256]{1,0:T(8,128)(2,1)S(1)}, u32[]{:S(2)}, u32[]{:S(2)}) collective-permute-start(bf16[512,256]{1,0:T(8,128)(2,1)S(1)} %get-tuple-element.39), channel_id=1, source_target_pairs={{2,0},{3,1},{4,2},{5,3},{6,4},{7,5},{8,6},{9,7},{10,8},{11,9},{12,... | collective-permute-start | bytes 786440 | tf_op jit(solution)/shard_map/ppermute | solution.py:27
  45.0 12.7 %collective-permute-start.7 = (bf16[512,256]{1,0:T(8,128)(2,1)S(1)}, bf16[512,256]{1,0:T(8,128)(2,1)S(1)}, u32[]{:S(2)}, u32[]{:S(2)}) collective-permute-start(bf16[512,256]{1,0:T(8,128)(2,1)S(1)} %get-tuple-element.43), channel_id=1, source_target_pairs={{2,0},{3,1},{4,2},{5,3},{6,4},{7,5},{8,6},{9,7},{10,8},{11,9},{12,... | collective-permute-start | bytes 786440 | tf_op jit(solution)/shard_map/ppermute | solution.py:27
  49.8 17.3 %collective-permute-start.9 = (bf16[256,256]{1,0:T(8,128)(2,1)S(1)}, bf16[256,256]{1,0:T(8,128)(2,1)S(1)}, u32[]{:S(2)}, u32[]{:S(2)}) collective-permute-start(bf16[256,256]{1,0:T(8,128)(2,1)S(1)} %get-tuple-element.59), channel_id=1, source_target_pairs={{1,0},{2,1},{3,2},{4,3},{5,4},{6,5},{7,6},{8,7},{9,8},{10,9},{11,1... | collective-permute-start | bytes 393224 | tf_op jit(solution)/shard_map/ppermute | solution.py:27
  54.4 12.8 %collective-permute-start.8 = (bf16[256,256]{1,0:T(8,128)(2,1)S(1)}, bf16[256,256]{1,0:T(8,128)(2,1)S(1)}, u32[]{:S(2)}, u32[]{:S(2)}) collective-permute-start(bf16[256,256]{1,0:T(8,128)(2,1)S(1)} %get-tuple-element.60), channel_id=1, source_target_pairs={{2,0},{3,1},{4,2},{5,3},{6,4},{7,5},{8,6},{9,7},{10,8},{11,9},{12,... | collective-permute-start | bytes 393224 | tf_op jit(solution)/shard_map/ppermute | solution.py:27
  57.8 9.4 %collective-permute-start.11 = (bf16[256,256]{1,0:T(8,128)(2,1)S(1)}, bf16[256,256]{1,0:T(8,128)(2,1)S(1)}, u32[]{:S(2)}, u32[]{:S(2)}) collective-permute-start(bf16[256,256]{1,0:T(8,128)(2,1)S(1)} %get-tuple-element.57), channel_id=1, source_target_pairs={{1,0},{2,1},{3,2},{4,3},{5,4},{6,5},{7,6},{8,7},{9,8},{10,9},{11,1... | collective-permute-start | bytes 393224 | tf_op jit(solution)/shard_map/ppermute | solution.py:27
  60.7 6.9 %collective-permute-start.10 = (bf16[256,256]{1,0:T(8,128)(2,1)S(1)}, bf16[256,256]{1,0:T(8,128)(2,1)S(1)}, u32[]{:S(2)}, u32[]{:S(2)}) collective-permute-start(bf16[256,256]{1,0:T(8,128)(2,1)S(1)} %get-tuple-element.58), channel_id=1, source_target_pairs={{2,0},{3,1},{4,2},{5,3},{6,4},{7,5},{8,6},{9,7},{10,8},{11,9},{12,... | collective-permute-start | bytes 393224 | tf_op jit(solution)/shard_map/ppermute | solution.py:27

commit v4 on v3

--- a/solution.py
+++ b/solution.py
@@ -69,7 +69,8 @@
         ref[pl.ds(first + i, 1), :] = value[:, i * tok : (i + 1) * tok]
 
 
-def near_stats_kernel(tok, group, kv_heads, offset, q_ref, g_ref, o_ref, own_ref, r1_ref, r2_ref, top_ref, sum_ref, delta_ref, bias_scr):
+def near_stats_kernel(tok, group, kv_heads, offset, q_ref, g_ref, o_ref, own_ref, r1_ref, r2_ref, top_ref, sum_ref, *rest):
+    *delta_refs, bias_scr = rest
     own = (own_ref, 0)
     pieces = ((r2_ref, 0), (r1_ref, 0), own)
     fill_bias(bias_scr, own, pieces, tok)
@@ -83,11 +84,15 @@
             top = jnp.max(s, axis=0, keepdims=True)
             put_stat(top_ref, first, top)
             put_stat(sum_ref, first, jnp.sum(jnp.exp2((s - top) * LOG2_SCALE), axis=0, keepdims=True))
-            prod = pair_rows(g_ref, offset + first).astype(jnp.float32) * pair_rows(o_ref, offset + first).astype(jnp.float32)
+        return carry
+
+    lax.fori_loop(0, kv_heads, one_kv_head, 0, unroll=True)
+    for c, delta_ref in enumerate(delta_refs):
+        heads = delta_ref.shape[0]
+        for first in range(0, heads, 2):
+            head = c * heads + first
+            prod = pair_rows(g_ref, head).astype(jnp.float32) * pair_rows(o_ref, head).astype(jnp.float32)
             put_stat(delta_ref, first, jnp.sum(prod.T, axis=0, keepdims=True))
-        return carry
-
-    lax.fori_loop(0, kv_heads, one_kv_head, 0, unroll=True)
 
 
 def gradients(ds, p, q_ref, g_ref, first, group):
@@ -245,13 +250,14 @@
         r43.append(shift(relayed, 2))
         near_out.append(call(
             near_stats_kernel, "near_stats", (query, out_grad, attn_out, own[c], r1[c], r2[c]),
-            (stat, stat, stat), (((near, tok), f32),), near, 1, sizes[c],
+            (stat, stat) + (stat,) * (CHUNKS if c == 0 else 0), (((near, tok), f32),), near, 1, sizes[c],
         ))
     pending = ((2 * tok, width), bf16)
     saved = ((far, heads * tok), bf16)
     far_out, x43 = [], []
     for c in parts:
-        near_top, near_sum, delta = near_out[c]
+        near_top, near_sum = near_out[c][:2]
+        delta = near_out[0][2 + c]
         far_out.append(call(
             far_kernel, "far_gradients", (query, out_grad, own[c], r43[c], near_top, near_sum, delta),
             (((4 * tok, width), bf16), stat, saved),
@@ -264,7 +270,7 @@
         if sums and not FULL2:
             lse, _ = lax.optimization_barrier((lse, sums[-1]))
         d2, d1, ds = call(
-            middle_kernel, "near_middle", (query, out_grad, own[c], r1[c], r2[c], lse, near_out[c][2]),
+            middle_kernel, "near_middle", (query, out_grad, own[c], r1[c], r2[c], lse, near_out[0][2 + c]),
             (pending, pending, saved), (((far, tok), f32), ((far, group * tok), bf16)), far, 4, sizes[c],
         )
         middle_ds.append(ds)
@@ -281,7 +287,7 @@
         lse, _ = lax.optimization_barrier((far_out[c][1], sums[-1]))
         query_grad, terms = call(
             own_kernel, "near_own",
-            (query, out_grad, own[c], r1[c], r2[c], r43[c], lse, near_out[c][2], far_out[c][2], middle_ds[c]),
+            (query, out_grad, own[c], r1[c], r2[c], r43[c], lse, near_out[0][2 + c], far_out[c][2], middle_ds[c]),
             (((tok, heads * HEAD_DIM), bf16), ((2 * tok, width), f32)),
             (((tok, tok), f32), ((tok, group * tok), bf16), ((tok, heads * tok), bf16)), tok, 9, sizes[c],
         )

time: 69 us -> 69.4 us (level)
  transfers between devices with their start and end apart: 12 -> 12, of which waited for: 6 -> 5; matrix products, arithmetic and copies ran while one was open for 2% -> 2% of each run, Pallas kernels for 18% -> 18%
where the time goes in v4:
time: 69.4 us; the launch traced here: 68.5 us
  starting transfers between devices  36.3 us (52%)
  waiting for transfers between devices  12.9 us (19%)
  Pallas kernels  12.2 us (18%)
  local copies, waits for them, and re-layouts  4.13 us (6%)
  other arithmetic  2.11 us (3%)
  between operations  0.89 us (1%)
    ppermute x12, starting transfers between devices, shift(): lax.ppermute(value, AXES, [(i, i + steps) for i in range(count) if 0 <= i...  36.3 us
    ppermute x12, waiting for transfers between devices, shift(): lax.ppermute(value, AXES, [(i, i + steps) for i in range(count) if 0 <= i...  12.9 us
    pallas_call x8, Pallas kernels, call(): pl.pallas_call(functools.partial(kernel, *sizes), in_specs=[whole] * len(...  12.2 us
    unnamed x6, local copies, waits for them, and re-layouts  2.45 us
  transfers between devices with their start and end apart: 12, of which 5 were waited for; matrix products, arithmetic and copies ran while one was open for 2% of the time, Pallas kernels for 18%

profile of v4, /device:TPU:6, one launch (start us, length us, event | category | flops | bytes accessed | tf_op | source)
XLA Modules:
  0.0 68.5 jit_solution(3974263561087287556)
XLA Ops:
  0.6 0.0 copy-start
  0.6 0.7 %add_convert_fusion.6 = bf16[128]{0:T(256)(128)(2,1)S(1)} fusion(s32[128]{0:T(128)} %param.11), kind=kLoop, calls=%fused_computation.12 | loop fusion | flops 256 | bytes 768 | tf_op jit(solution)/shard_map/convert_element_type | solution.py:230
  1.4 1.0 %fusion.1 = (bf16[128,256]{1,0:T(8,128)(2,1)S(1)}, bf16[128,256]{1,0:T(8,128)(2,1)S(1)}, bf16[128,256]{1,0:T(8,128)(2,1)S(1)}, bf16[128,256]{1,0:T(8,128)(2,1)S(1)}) fusion(bf16[128,512]{1,0:T(8,128)(2,1)} %param.7, bf16[128,512]{1,0:T(8,128)(2,1)} %param.8), kind=kLoop, calls=%fused_computation.15 | loop fusion | bytes 524288 | tf_op jit(solution)/shard_map/slice | solution.py:242
  2.4 3.8 %collective-permute-start.1 = (bf16[272,256]{1,0:T(8,128)(2,1)S(1)}, bf16[272,256]{1,0:T(8,128)(2,1)S(1)}, u32[]{:S(2)}, u32[]{:S(2)}) collective-permute-start(bf16[272,256]{1,0:T(8,128)(2,1)S(1)} %get-tuple-element.65.own_ref), channel_id=1, source_target_pairs={{0,2},{1,3},{2,4},{3,5},{4,6},{5,7},{6,8},{7,9},{8,10},{9,11},{10,... | collective-permute-start | bytes 417800 | tf_op jit(solution)/shard_map/ppermute | solution.py:27
  6.2 3.5 %collective-permute-start = (bf16[272,256]{1,0:T(8,128)(2,1)S(1)}, bf16[272,256]{1,0:T(8,128)(2,1)S(1)}, u32[]{:S(2)}, u32[]{:S(2)}) collective-permute-start(bf16[272,256]{1,0:T(8,128)(2,1)S(1)} %get-tuple-element.65.own_ref), channel_id=1, source_target_pairs={{0,1},{1,2},{2,3},{3,4},{4,5},{5,6},{6,7},{7,8},{8,9},{9,10},{10,1... | collective-permute-start | bytes 417800 | tf_op jit(solution)/shard_map/ppermute | solution.py:27
  9.7 3.8 %collective-permute-start.4 = (bf16[272,256]{1,0:T(8,128)(2,1)S(1)}, bf16[272,256]{1,0:T(8,128)(2,1)S(1)}, u32[]{:S(2)}, u32[]{:S(2)}) collective-permute-start(bf16[272,256]{1,0:T(8,128)(2,1)S(1)} %get-tuple-element.66.own_ref), channel_id=1, source_target_pairs={{0,2},{1,3},{2,4},{3,5},{4,6},{5,7},{6,8},{7,9},{8,10},{9,11},{10,... | collective-permute-start | bytes 417800 | tf_op jit(solution)/shard_map/ppermute | solution.py:27
  13.6 3.7 %collective-permute-start.3 = (bf16[272,256]{1,0:T(8,128)(2,1)S(1)}, bf16[272,256]{1,0:T(8,128)(2,1)S(1)}, u32[]{:S(2)}, u32[]{:S(2)}) collective-permute-start(bf16[272,256]{1,0:T(8,128)(2,1)S(1)} %get-tuple-element.66.own_ref), channel_id=1, source_target_pairs={{0,1},{1,2},{2,3},{3,4},{4,5},{5,6},{6,7},{7,8},{8,9},{9,10},{10,1... | collective-permute-start | bytes 417800 | tf_op jit(solution)/shard_map/ppermute | solution.py:27
  17.3 2.2 %collective-permute-done.1.r2_ref = bf16[272,256]{1,0:T(8,128)(2,1)S(1)} collective-permute-done((bf16[272,256]{1,0:T(8,128)(2,1)S(1)}, bf16[272,256]{1,0:T(8,128)(2,1)S(1)}, u32[]{:S(2)}, u32[]{:S(2)}) %collective-permute-start.1) | collective-permute-done | bytes 139296 | tf_op jit(solution)/shard_map/ppermute | solution.py:27
  19.5 2.8 %collective-permute-done.r1_ref = bf16[272,256]{1,0:T(8,128)(2,1)S(1)} collective-permute-done((bf16[272,256]{1,0:T(8,128)(2,1)S(1)}, bf16[272,256]{1,0:T(8,128)(2,1)S(1)}, u32[]{:S(2)}, u32[]{:S(2)}) %collective-permute-start) | collective-permute-done | bytes 139296 | tf_op jit(solution)/shard_map/ppermute | solution.py:27
  22.3 1.9 %collective-permute-start.2 = (bf16[544,256]{1,0:T(8,128)(2,1)S(1)}, bf16[544,256]{1,0:T(8,128)(2,1)S(1)}, u32[]{:S(2)}, u32[]{:S(2)}) collective-permute-start(bf16[544,256]{1,0:T(8,128)(2,1)S(1)} %pad_maximum_fusion.1), channel_id=1, source_target_pairs={{0,2},{1,3},{2,4},{3,5},{4,6},{5,7},{6,8},{7,9},{8,10},{9,11},{10,... | collective-permute-start | bytes 835592 | tf_op jit(solution)/shard_map/ppermute | solution.py:27
  24.3 0.0 copy-done
  24.3 0.0 copy-start.1
  24.3 1.2 %copy-done.1 = bf16[128,4096]{1,0:T(8,128)(2,1)S(1)} copy-done((bf16[128,4096]{1,0:T(8,128)(2,1)S(1)}, bf16[128,4096]{1,0:T(8,128)(2,1)}, u32[]{:S(2)}) %copy-start.1) | copy-done | bytes 1048600
  25.5 0.0 copy-start.2
  25.5 1.2 %copy-done.2 = bf16[128,4096]{1,0:T(8,128)(2,1)S(1)} copy-done((bf16[128,4096]{1,0:T(8,128)(2,1)S(1)}, bf16[128,4096]{1,0:T(8,128)(2,1)}, u32[]{:S(2)}) %copy-start.2) | copy-done | bytes 1048600
  26.7 1.4 %near_stats.2 = (f32[16,128]{1,0:T(8,128)S(1)}, f32[16,128]{1,0:T(8,128)S(1)}, f32[16,128]{1,0:T(8,128)S(1)}, f32[16,128]{1,0:T(8,128)S(1)}) custom-call(bf16[128,4096]{1,0:T(8,128)(2,1)S(1)} %copy-done, bf16[128,4096]{1,0:T(8,128)(2,1)S(1)} %copy-done.1, bf16[128,4096]{1,0:T(8,128)(2,1)S(1)} %copy-done.2, bf16[272,256]{1,0:T(8,128)(2,1)S(1)} %get-tuple-element.65.own_ref, ...), custom_call_target="tpu_custom_call" | custom-call | flops 201326592 | bytes 3563520 | tf_op jit(solution)/shard_map/near_stats/pallas_call | solution.py:209
  28.1 0.0 collective-permute-done.4.r2_ref
  28.1 0.1 collective-permute-done.3.r1_ref
  28.3 1.9 %collective-permute-start.5 = (bf16[544,256]{1,0:T(8,128)(2,1)S(1)}, bf16[544,256]{1,0:T(8,128)(2,1)S(1)}, u32[]{:S(2)}, u32[]{:S(2)}) collective-permute-start(bf16[544,256]{1,0:T(8,128)(2,1)S(1)} %pad_maximum_fusion.2), channel_id=1, source_target_pairs={{0,2},{1,3},{2,4},{3,5},{4,6},{5,7},{6,8},{7,9},{8,10},{9,11},{10,... | collective-permute-start | bytes 835592 | tf_op jit(solution)/shard_map/ppermute | solution.py:27
  30.2 6.8 %collective-permute-done.2.far_ref = bf16[544,256]{1,0:T(8,128)(2,1)S(1)} collective-permute-done((bf16[544,256]{1,0:T(8,128)(2,1)S(1)}, bf16[544,256]{1,0:T(8,128)(2,1)S(1)}, u32[]{:S(2)}, u32[]{:S(2)}) %collective-permute-start.2) | collective-permute-done | bytes 278560 | tf_op jit(solution)/shard_map/ppermute | solution.py:27
  37.0 2.1 %far_gradients.2 = (bf16[512,256]{1,0:T(8,128)(2,1)S(1)}, f32[16,128]{1,0:T(8,128)S(1)}, bf16[256,2048]{1,0:T(8,128)(2,1)S(1)}) custom-call(bf16[128,4096]{1,0:T(8,128)(2,1)S(1)} %copy-done, bf16[128,4096]{1,0:T(8,128)(2,1)S(1)} %copy-done.1, bf16[272,256]{1,0:T(8,128)(2,1)S(1)} %get-tuple-element.65.own_ref, ...), custom_call_target="tpu_custom_call" | custom-call | flops 536870912 | bytes 2539520 | tf_op jit(solution)/shard_map/far_gradients/pallas_call | solution.py:209
  39.1 1.9 %collective-permute-start.6 = (bf16[512,256]{1,0:T(8,128)(2,1)S(1)}, bf16[512,256]{1,0:T(8,128)(2,1)S(1)}, u32[]{:S(2)}, u32[]{:S(2)}) collective-permute-start(bf16[512,256]{1,0:T(8,128)(2,1)S(1)} %get-tuple-element.39), channel_id=1, source_target_pairs={{2,0},{3,1},{4,2},{5,3},{6,4},{7,5},{8,6},{9,7},{10,8},{11,9},{12,... | collective-permute-start | bytes 786440 | tf_op jit(solution)/shard_map/ppermute | solution.py:27
  41.0 1.0 %near_stats.3 = (f32[16,128]{1,0:T(8,128)S(1)}, f32[16,128]{1,0:T(8,128)S(1)}) custom-call(bf16[128,4096]{1,0:T(8,128)(2,1)S(1)} %copy-done, bf16[128,4096]{1,0:T(8,128)(2,1)S(1)} %copy-done.1, bf16[128,4096]{1,0:T(8,128)(2,1)S(1)} %copy-done.2, bf16[272,256]{1,0:T(8,128)(2,1)S(1)} %get-tuple-element.66.own_ref, ...), custom_call_target="tpu_custom_call" | custom-call | flops 201326592 | bytes 3563520 | tf_op jit(solution)/shard_map/near_stats/pallas_call | solution.py:209
  42.1 0.8 %collective-permute-done.5.far_ref = bf16[544,256]{1,0:T(8,128)(2,1)S(1)} collective-permute-done((bf16[544,256]{1,0:T(8,128)(2,1)S(1)}, bf16[544,256]{1,0:T(8,128)(2,1)S(1)}, u32[]{:S(2)}, u32[]{:S(2)}) %collective-permute-start.5) | collective-permute-done | bytes 278560 | tf_op jit(solution)/shard_map/ppermute | solution.py:27
  42.9 2.1 %far_gradients.3 = (bf16[512,256]{1,0:T(8,128)(2,1)S(1)}, f32[16,128]{1,0:T(8,128)S(1)}, bf16[256,2048]{1,0:T(8,128)(2,1)S(1)}) custom-call(bf16[128,4096]{1,0:T(8,128)(2,1)S(1)} %copy-done, bf16[128,4096]{1,0:T(8,128)(2,1)S(1)} %copy-done.1, bf16[272,256]{1,0:T(8,128)(2,1)S(1)} %get-tuple-element.66.own_ref, ...), custom_call_target="tpu_custom_call" | custom-call | flops 536870912 | bytes 2539520 | tf_op jit(solution)/shard_map/far_gradients/pallas_call | solution.py:209
  45.0 3.5 %collective-permute-start.7 = (bf16[512,256]{1,0:T(8,128)(2,1)S(1)}, bf16[512,256]{1,0:T(8,128)(2,1)S(1)}, u32[]{:S(2)}, u32[]{:S(2)}) collective-permute-start(bf16[512,256]{1,0:T(8,128)(2,1)S(1)} %get-tuple-element.43), channel_id=1, source_target_pairs={{2,0},{3,1},{4,2},{5,3},{6,4},{7,5},{8,6},{9,7},{10,8},{11,9},{12,... | collective-permute-start | bytes 786440 | tf_op jit(solution)/shard_map/ppermute | solution.py:27
  48.5 1.4 %near_middle.2 = (bf16[256,256]{1,0:T(8,128)(2,1)S(1)}, bf16[256,256]{1,0:T(8,128)(2,1)S(1)}, bf16[256,2048]{1,0:T(8,128)(2,1)S(1)}) custom-call(bf16[128,4096]{1,0:T(8,128)(2,1)S(1)} %copy-done, bf16[128,4096]{1,0:T(8,128)(2,1)S(1)} %copy-done.1, bf16[272,256]{1,0:T(8,128)(2,1)S(1)} %get-tuple-element.65.own_ref, ...), custom_call_target="tpu_custom_call" | custom-call | flops 536870912 | bytes 2531328 | tf_op jit(solution)/shard_map/near_middle/pallas_call | solution.py:209
  49.9 0.0 collective-permute-done.6
  49.9 0.1 add_convert_fusion.4
  50.0 4.4 %collective-permute-start.9 = (bf16[256,256]{1,0:T(8,128)(2,1)S(1)}, bf16[256,256]{1,0:T(8,128)(2,1)S(1)}, u32[]{:S(2)}, u32[]{:S(2)}) collective-permute-start(bf16[256,256]{1,0:T(8,128)(2,1)S(1)} %get-tuple-element.59), channel_id=1, source_target_pairs={{1,0},{2,1},{3,2},{4,3},{5,4},{6,5},{7,6},{8,7},{9,8},{10,9},{11,1... | collective-permute-start | bytes 393224 | tf_op jit(solution)/shard_map/ppermute | solution.py:27
  54.4 1.9 %collective-permute-start.8 = (bf16[256,256]{1,0:T(8,128)(2,1)S(1)}, bf16[256,256]{1,0:T(8,128)(2,1)S(1)}, u32[]{:S(2)}, u32[]{:S(2)}) collective-permute-start(bf16[256,256]{1,0:T(8,128)(2,1)S(1)} %get-tuple-element.60), channel_id=1, source_target_pairs={{2,0},{3,1},{4,2},{5,3},{6,4},{7,5},{8,6},{9,7},{10,8},{11,9},{12,... | collective-permute-start | bytes 393224 | tf_op jit(solution)/shard_map/ppermute | solution.py:27
  56.3 1.4 %near_middle.3 = (bf16[256,256]{1,0:T(8,128)(2,1)S(1)}, bf16[256,256]{1,0:T(8,128)(2,1)S(1)}, bf16[256,2048]{1,0:T(8,128)(2,1)S(1)}) custom-call(bf16[128,4096]{1,0:T(8,128)(2,1)S(1)} %copy-done, bf16[128,4096]{1,0:T(8,128)(2,1)S(1)} %copy-done.1, bf16[272,256]{1,0:T(8,128)(2,1)S(1)} %get-tuple-element.66.own_ref, ...), custom_call_target="tpu_custom_call" | custom-call | flops 536870912 | bytes 2531328 | tf_op jit(solution)/shard_map/near_middle/pallas_call | solution.py:209
  57.7 0.0 collective-permute-done.7
  57.7 0.1 add_convert_fusion.2
  57.8 2.7 %collective-permute-start.11 = (bf16[256,256]{1,0:T(8,128)(2,1)S(1)}, bf16[256,256]{1,0:T(8,128)(2,1)S(1)}, u32[]{:S(2)}, u32[]{:S(2)}) collective-permute-start(bf16[256,256]{1,0:T(8,128)(2,1)S(1)} %get-tuple-element.57), channel_id=1, source_target_pairs={{1,0},{2,1},{3,2},{4,3},{5,4},{6,5},{7,6},{8,7},{9,8},{10,9},{11,1... | collective-permute-start | bytes 393224 | tf_op jit(solution)/shard_map/ppermute | solution.py:27
  60.5 3.2 %collective-permute-start.10 = (bf16[256,256]{1,0:T(8,128)(2,1)S(1)}, bf16[256,256]{1,0:T(8,128)(2,1)S(1)}, u32[]{:S(2)}, u32[]{:S(2)}) collective-permute-start(bf16[256,256]{1,0:T(8,128)(2,1)S(1)} %get-tuple-element.58), channel_id=1, source_target_pairs={{2,0},{3,1},{4,2},{5,3},{6,4},{7,5},{8,6},{9,7},{10,8},{11,9},{12,... | collective-permute-start | bytes 393224 | tf_op jit(solution)/shard_map/ppermute | solution.py:27
  63.7 1.4 %near_own.3 = (bf16[128,2048]{1,0:T(8,128)(2,1)S(1)}, f32[256,256]{1,0:T(8,128)S(1)}) custom-call(bf16[128,4096]{1,0:T(8,128)(2,1)S(1)} %copy-done, bf16[128,4096]{1,0:T(8,128)(2,1)S(1)} %copy-done.1, bf16[272,256]{1,0:T(8,128)(2,1)S(1)} %get-tuple-element.66.own_ref, bf16[272,256]{1,0:T(8,128)(2,1)S(1)} %collective-permute-done.3.r1_ref, ...), custom_call_target="tpu_custom_call" | custom-call | flops 603979776 | bytes 4907008 | tf_op jit(solution)/shard_map/near_own/pallas_call | solution.py:209
  65.1 1.4 %near_own.2 = (bf16[128,2048]{1,0:T(8,128)(2,1)S(1)}, f32[256,256]{1,0:T(8,128)S(1)}) custom-call(bf16[128,4096]{1,0:T(8,128)(2,1)S(1)} %copy-done, bf16[128,4096]{1,0:T(8,128)(2,1)S(1)} %copy-done.1, bf16[272,256]{1,0:T(8,128)(2,1)S(1)} %get-tuple-element.65.own_ref, bf16[272,256]{1,0:T(8,128)(2,1)S(1)} %collective-permute-done.r1_ref, ...), custom_call_target="tpu_custom_call" | custom-call | flops 603979776 | bytes 4907008 | tf_op jit(solution)/shard_map/near_own/pallas_call | solution.py:209
  66.6 1.0 %pad_maximum_fusion = bf16[128,4096]{1,0:T(8,128)(2,1)} fusion(bf16[128,2048]{1,0:T(8,128)(2,1)S(1)} %get-tuple-element.52, bf16[128,2048]{1,0:T(8,128)(2,1)S(1)} %get-tuple-element.48), kind=kLoop, calls=%fused_computation | loop fusion | flops 2097152 | bytes 2097152 | tf_op jit(solution)/shard_map/concatenate | solution.py:300
  67.6 0.0 collective-permute-done.9
  67.6 0.0 collective-permute-done.8
  67.6 0.1 add_convert_fusion.1
  67.7 0.0 collective-permute-done.11
  67.7 0.0 collective-permute-done.10
  67.8 0.7 %fusion = (bf16[128,512]{1,0:T(8,128)(2,1)}, bf16[128,512]{1,0:T(8,128)(2,1)}) fusion(bf16[256,512]{1,0:T(8,128)(2,1)S(1)} %pad_maximum_fusion.3), kind=kLoop, calls=%fused_computation.14 | loop fusion | bytes 524288 | tf_op jit(solution)/shard_map/slice | solution.py:300
  (7 shorter events, 0.1 us)
Async XLA Ops:
  0.6 23.6 %copy-start = (bf16[128,4096]{1,0:T(8,128)(2,1)S(1)}, bf16[128,4096]{1,0:T(8,128)(2,1)}, u32[]{:S(2)}) copy-start(bf16[128,4096]{1,0:T(8,128)(2,1)} %q_ref.15) | copy-start | bytes 3145732
  2.4 17.1 %collective-permute-start.1 = (bf16[272,256]{1,0:T(8,128)(2,1)S(1)}, bf16[272,256]{1,0:T(8,128)(2,1)S(1)}, u32[]{:S(2)}, u32[]{:S(2)}) collective-permute-start(bf16[272,256]{1,0:T(8,128)(2,1)S(1)} %get-tuple-element.65.own_ref), channel_id=1, source_target_pairs={{0,2},{1,3},{2,4},{3,5},{4,6},{5,7},{6,8},{7,9},{8,10},{9,11},{10,... | collective-permute-start | bytes 417800 | tf_op jit(solution)/shard_map/ppermute | solution.py:27
  6.2 16.1 %collective-permute-start = (bf16[272,256]{1,0:T(8,128)(2,1)S(1)}, bf16[272,256]{1,0:T(8,128)(2,1)S(1)}, u32[]{:S(2)}, u32[]{:S(2)}) collective-permute-start(bf16[272,256]{1,0:T(8,128)(2,1)S(1)} %get-tuple-element.65.own_ref), channel_id=1, source_target_pairs={{0,1},{1,2},{2,3},{3,4},{4,5},{5,6},{6,7},{7,8},{8,9},{9,10},{10,1... | collective-permute-start | bytes 417800 | tf_op jit(solution)/shard_map/ppermute | solution.py:27
  9.7 18.4 %collective-permute-start.4 = (bf16[272,256]{1,0:T(8,128)(2,1)S(1)}, bf16[272,256]{1,0:T(8,128)(2,1)S(1)}, u32[]{:S(2)}, u32[]{:S(2)}) collective-permute-start(bf16[272,256]{1,0:T(8,128)(2,1)S(1)} %get-tuple-element.66.own_ref), channel_id=1, source_target_pairs={{0,2},{1,3},{2,4},{3,5},{4,6},{5,7},{6,8},{7,9},{8,10},{9,11},{10,... | collective-permute-start | bytes 417800 | tf_op jit(solution)/shard_map/ppermute | solution.py:27
  13.6 14.7 %collective-permute-start.3 = (bf16[272,256]{1,0:T(8,128)(2,1)S(1)}, bf16[272,256]{1,0:T(8,128)(2,1)S(1)}, u32[]{:S(2)}, u32[]{:S(2)}) collective-permute-start(bf16[272,256]{1,0:T(8,128)(2,1)S(1)} %get-tuple-element.66.own_ref), channel_id=1, source_target_pairs={{0,1},{1,2},{2,3},{3,4},{4,5},{5,6},{6,7},{7,8},{8,9},{9,10},{10,1... | collective-permute-start | bytes 417800 | tf_op jit(solution)/shard_map/ppermute | solution.py:27
  22.3 14.7 %collective-permute-start.2 = (bf16[544,256]{1,0:T(8,128)(2,1)S(1)}, bf16[544,256]{1,0:T(8,128)(2,1)S(1)}, u32[]{:S(2)}, u32[]{:S(2)}) collective-permute-start(bf16[544,256]{1,0:T(8,128)(2,1)S(1)} %pad_maximum_fusion.1), channel_id=1, source_target_pairs={{0,2},{1,3},{2,4},{3,5},{4,6},{5,7},{6,8},{7,9},{8,10},{9,11},{10,... | collective-permute-start | bytes 835592 | tf_op jit(solution)/shard_map/ppermute | solution.py:27
  24.3 1.2 %copy-start.1 = (bf16[128,4096]{1,0:T(8,128)(2,1)S(1)}, bf16[128,4096]{1,0:T(8,128)(2,1)}, u32[]{:S(2)}) copy-start(bf16[128,4096]{1,0:T(8,128)(2,1)} %g_ref.15) | copy-start | bytes 3145732
  25.5 1.2 %copy-start.2 = (bf16[128,4096]{1,0:T(8,128)(2,1)S(1)}, bf16[128,4096]{1,0:T(8,128)(2,1)}, u32[]{:S(2)}) copy-start(bf16[128,4096]{1,0:T(8,128)(2,1)} %o_ref.3) | copy-start | bytes 3145732
  28.3 14.6 %collective-permute-start.5 = (bf16[544,256]{1,0:T(8,128)(2,1)S(1)}, bf16[544,256]{1,0:T(8,128)(2,1)S(1)}, u32[]{:S(2)}, u32[]{:S(2)}) collective-permute-start(bf16[544,256]{1,0:T(8,128)(2,1)S(1)} %pad_maximum_fusion.2), channel_id=1, source_target_pairs={{0,2},{1,3},{2,4},{3,5},{4,6},{5,7},{6,8},{7,9},{8,10},{9,11},{10,... | collective-permute-start | bytes 835592 | tf_op jit(solution)/shard_map/ppermute | solution.py:27
  39.1 10.8 %collective-permute-start.6 = (bf16[512,256]{1,0:T(8,128)(2,1)S(1)}, bf16[512,256]{1,0:T(8,128)(2,1)S(1)}, u32[]{:S(2)}, u32[]{:S(2)}) collective-permute-start(bf16[512,256]{1,0:T(8,128)(2,1)S(1)} %get-tuple-element.39), channel_id=1, source_target_pairs={{2,0},{3,1},{4,2},{5,3},{6,4},{7,5},{8,6},{9,7},{10,8},{11,9},{12,... | collective-permute-start | bytes 786440 | tf_op jit(solution)/shard_map/ppermute | solution.py:27
  45.0 12.7 %collective-permute-start.7 = (bf16[512,256]{1,0:T(8,128)(2,1)S(1)}, bf16[512,256]{1,0:T(8,128)(2,1)S(1)}, u32[]{:S(2)}, u32[]{:S(2)}) collective-permute-start(bf16[512,256]{1,0:T(8,128)(2,1)S(1)} %get-tuple-element.43), channel_id=1, source_target_pairs={{2,0},{3,1},{4,2},{5,3},{6,4},{7,5},{8,6},{9,7},{10,8},{11,9},{12,... | collective-permute-start | bytes 786440 | tf_op jit(solution)/shard_map/ppermute | solution.py:27
  50.0 17.6 %collective-permute-start.9 = (bf16[256,256]{1,0:T(8,128)(2,1)S(1)}, bf16[256,256]{1,0:T(8,128)(2,1)S(1)}, u32[]{:S(2)}, u32[]{:S(2)}) collective-permute-start(bf16[256,256]{1,0:T(8,128)(2,1)S(1)} %get-tuple-element.59), channel_id=1, source_target_pairs={{1,0},{2,1},{3,2},{4,3},{5,4},{6,5},{7,6},{8,7},{9,8},{10,9},{11,1... | collective-permute-start | bytes 393224 | tf_op jit(solution)/shard_map/ppermute | solution.py:27
  54.4 13.2 %collective-permute-start.8 = (bf16[256,256]{1,0:T(8,128)(2,1)S(1)}, bf16[256,256]{1,0:T(8,128)(2,1)S(1)}, u32[]{:S(2)}, u32[]{:S(2)}) collective-permute-start(bf16[256,256]{1,0:T(8,128)(2,1)S(1)} %get-tuple-element.60), channel_id=1, source_target_pairs={{2,0},{3,1},{4,2},{5,3},{6,4},{7,5},{8,6},{9,7},{10,8},{11,9},{12,... | collective-permute-start | bytes 393224 | tf_op jit(solution)/shard_map/ppermute | solution.py:27
  57.8 9.9 %collective-permute-start.11 = (bf16[256,256]{1,0:T(8,128)(2,1)S(1)}, bf16[256,256]{1,0:T(8,128)(2,1)S(1)}, u32[]{:S(2)}, u32[]{:S(2)}) collective-permute-start(bf16[256,256]{1,0:T(8,128)(2,1)S(1)} %get-tuple-element.57), channel_id=1, source_target_pairs={{1,0},{2,1},{3,2},{4,3},{5,4},{6,5},{7,6},{8,7},{9,8},{10,9},{11,1... | collective-permute-start | bytes 393224 | tf_op jit(solution)/shard_map/ppermute | solution.py:27
  60.5 7.2 %collective-permute-start.10 = (bf16[256,256]{1,0:T(8,128)(2,1)S(1)}, bf16[256,256]{1,0:T(8,128)(2,1)S(1)}, u32[]{:S(2)}, u32[]{:S(2)}) collective-permute-start(bf16[256,256]{1,0:T(8,128)(2,1)S(1)} %get-tuple-element.58), channel_id=1, source_target_pairs={{2,0},{3,1},{4,2},{5,3},{6,4},{7,5},{8,6},{9,7},{10,8},{11,9},{12,... | collective-permute-start | bytes 393224 | tf_op jit(solution)/shard_map/ppermute | solution.py:27
